TPU v7x, 256 devices: a whole 4x4x8 slice. The times are simulated.
256 devices in a mesh: grp: 8 (over y_lo, x), ctx: 32 (over y_hi, z, core).
Axes of the slice: x: 4, y: 4 (y_hi: 2, y_lo: 2; y = y_hi * 2 + y_lo), z: 8, core: 2. Of those that a mesh axis runs over, the one named last changes fastest.
Arguments:
- query_rows: bfloat16 [32768, 4096], P(('grp', 'ctx')), may hold values from -6 to 6
- key_rows: bfloat16 [32768, 512], P(('grp', 'ctx')), may hold values from -6 to 6
- value_rows: bfloat16 [32768, 512], P(('grp', 'ctx')), may hold values from -6 to 6
- output_grad: bfloat16 [32768, 4096], P(('grp', 'ctx')), may hold values from -6 to 6
- block_target: int32 [8, 32, 16], replicated, may hold values from 0 to 4095, as said below
- doc_lengths: int32 [8, 16], P('grp'), may hold values from 1 to 512, 4096 in all within a row
Outputs:
- query_grad: bfloat16 [32768, 4096], P(('grp', 'ctx'))
- key_grad: bfloat16 [32768, 512], P(('grp', 'ctx'))
- value_grad: bfloat16 [32768, 512], P(('grp', 'ctx'))
Inputs may be any that keep to these rules, and one draw needn't show every extreme that they name: `block_target`: all entries together are a permutation of the packed blocks. Slot j of every loader device targets packed group j // 2. Of the slots that the devices with one ctx index (over all groups) send to one packed group, at most 1 target any one device of it. `doc_lengths`: each row sums to 4096.
All inputs are finite; a program needn't handle non-finite values.
Results may differ from a plain program's by a relative error of at most 0.012.
Values may be sent and summed in bfloat16 or wider, within the bound.
A program may use at most 128 MiB of HBM per device.

v0:
```python
import jax
import jax.numpy as jnp
from jax import lax
from jax.sharding import PartitionSpec as P

KV_HEADS = 4
HEAD_DIM = 128
TOK_DEV = 128
BLOCK_ROWS = 8
REACH = 4
SHARE = 8
BLOCKS_DEV = 16


def shifted(shard, axis, by):
    devices = lax.axis_size(axis)
    pairs = [(i, i + by) for i in range(devices) if 0 <= i + by < devices]
    return lax.ppermute(shard, axis, pairs)


def shifted_2(block, axis, distance):
    devices = range(lax.axis_size(axis))
    route = [((i - distance) % len(devices), i) for i in devices]
    return lax.ppermute(block, axis, route)


def doc_index(doc_ends, positions):
    return jnp.sum((doc_ends[None, :] <= positions[:, None]).astype(jnp.int32), axis=1)


def earlier_count(targets):
    slot_order = jnp.arange(targets.shape[-1])
    same_target = targets[..., :, None] == targets[..., None, :]
    earlier_slot = slot_order[None, :] < slot_order[:, None]
    return jnp.sum((same_target & earlier_slot).astype(jnp.int32), axis=-1)


def routing(block_target, group_index, member_index, groups, members):
    per_group = BLOCKS_DEV // groups
    capacity = max(1, BLOCKS_DEV // members)
    group_offset = group_index * BLOCKS_DEV * members
    held_all = lax.dynamic_slice(
        block_target, (0, 0, group_index * per_group), (groups, members, per_group)
    )
    held_all = jnp.transpose(held_all, (1, 0, 2)).reshape(members, BLOCKS_DEV) - group_offset
    target_dev = held_all // BLOCKS_DEV
    target_slot = held_all % BLOCKS_DEV
    slot_rank = earlier_count(target_dev)
    my_targets = lax.dynamic_index_in_dim(target_dev, member_index, 0, keepdims=False)
    my_ranks = lax.dynamic_index_in_dim(slot_rank, member_index, 0, keepdims=False)
    send_slot = my_targets * capacity + my_ranks
    send_table = (jnp.arange(members * capacity)[:, None] == send_slot[None, :]).astype(
        jnp.bfloat16
    )
    arrives_here = (target_dev == member_index)[None, :, :, None]
    slot_match = target_slot[None, :, :, None] == jnp.arange(BLOCKS_DEV)[:, None, None, None]
    rank_match = slot_rank[None, :, :, None] == jnp.arange(capacity)[None, None, None, :]
    recv_hits = jnp.sum((arrives_here & slot_match & rank_match).astype(jnp.int32), axis=2)
    recv_table = recv_hits.reshape(BLOCKS_DEV, members * capacity).astype(jnp.bfloat16)
    return (send_table, recv_table)


def apply_table(table, block_view):
    return jnp.dot(table, block_view, preferred_element_type=jnp.float32).astype(jnp.bfloat16)


def apply_transposed(table, block_view):
    return jnp.einsum("ab,ac->bc", table, block_view, preferred_element_type=jnp.float32).astype(
        jnp.bfloat16
    )


def tile_allowed(doc_ends, query_pos, root):
    key_pos = root * TOK_DEV + jnp.arange(TOK_DEV, dtype=jnp.int32)
    same_doc = doc_index(doc_ends, query_pos)[:, None] == doc_index(doc_ends, key_pos)[None, :]
    return same_doc & (key_pos[None, :] <= query_pos[:, None]) & (root >= 0)


def on_device(query_rows, key_rows, value_rows, output_grad, block_target, doc_lengths):
    groups = lax.axis_size("grp")
    members = lax.axis_size("ctx")
    group_index = lax.axis_index("grp")
    member_index = lax.axis_index("ctx")
    per_group = BLOCKS_DEV // groups
    capacity = max(1, BLOCKS_DEV // members)
    query_width = query_rows.shape[1]
    pair_width = key_rows.shape[1]
    arrived = (
        lax.all_to_all(
            query_rows.reshape(groups, per_group * BLOCK_ROWS, query_width),
            "grp",
            split_axis=0,
            concat_axis=0,
            tiled=True,
        ),
        lax.all_to_all(
            key_rows.reshape(groups, per_group * BLOCK_ROWS, pair_width),
            "grp",
            split_axis=0,
            concat_axis=0,
            tiled=True,
        ),
        lax.all_to_all(
            value_rows.reshape(groups, per_group * BLOCK_ROWS, pair_width),
            "grp",
            split_axis=0,
            concat_axis=0,
            tiled=True,
        ),
        lax.all_to_all(
            output_grad.reshape(groups, per_group * BLOCK_ROWS, query_width),
            "grp",
            split_axis=0,
            concat_axis=0,
            tiled=True,
        ),
    )
    send_table, recv_table = routing(block_target, group_index, member_index, groups, members)

    def to_slots(source):
        row_width = source.shape[-1]
        block_view = source.reshape(BLOCKS_DEV, BLOCK_ROWS * row_width)
        return apply_table(send_table, block_view).reshape(
            members, capacity * BLOCK_ROWS, row_width
        )

    def from_slots(source):
        row_width = source.shape[-1]
        block_view = source.reshape(members * capacity, BLOCK_ROWS * row_width)
        return apply_table(recv_table, block_view).reshape(TOK_DEV, row_width)

    delivered = (
        lax.all_to_all(to_slots(arrived[0]), "ctx", split_axis=0, concat_axis=0, tiled=True),
        lax.all_to_all(to_slots(arrived[1]), "ctx", split_axis=0, concat_axis=0, tiled=True),
        lax.all_to_all(to_slots(arrived[2]), "ctx", split_axis=0, concat_axis=0, tiled=True),
        lax.all_to_all(to_slots(arrived[3]), "ctx", split_axis=0, concat_axis=0, tiled=True),
    )
    query_pack = from_slots(delivered[0]).reshape(TOK_DEV, KV_HEADS, SHARE, HEAD_DIM)
    key_pack = from_slots(delivered[1]).reshape(TOK_DEV, KV_HEADS, HEAD_DIM)
    value_pack = from_slots(delivered[2]).reshape(TOK_DEV, KV_HEADS, HEAD_DIM)
    grad_pack = from_slots(delivered[3]).reshape(TOK_DEV, KV_HEADS, SHARE, HEAD_DIM)
    doc_ends = jnp.cumsum(doc_lengths[0])
    query_pos = member_index * TOK_DEV + jnp.arange(TOK_DEV, dtype=jnp.int32)
    allowed = [
        tile_allowed(doc_ends, query_pos, member_index - offset) for offset in range(REACH + 1)
    ]
    score_scale = HEAD_DIM ** (-0.5)

    def scores_of(key_block):
        return (
            jnp.einsum("ihgd,jhd->hgij", query_pack, key_block, preferred_element_type=jnp.float32)
            * score_scale
        )

    def stats_tile(state_pair, key_block, tile_mask):
        row_max, row_sum = state_pair
        scores = scores_of(key_block)
        new_max = jnp.maximum(
            row_max, jnp.max(jnp.where(tile_mask, scores, -jnp.inf), axis=-1, keepdims=True)
        )
        new_sum = row_sum * jnp.exp(row_max - new_max) + jnp.sum(
            jnp.where(tile_mask, jnp.exp(scores - new_max), 0.0), axis=-1, keepdims=True
        )
        return (new_max, new_sum)

    def output_tile(out_sum, key_block, value_block, tile_mask, log_total):
        weights_low = jnp.where(tile_mask, jnp.exp(scores_of(key_block) - log_total), 0.0).astype(
            jnp.bfloat16
        )
        return out_sum + jnp.einsum(
            "hgij,jhd->ihgd", weights_low, value_block, preferred_element_type=jnp.float32
        )

    start_state = (
        jnp.full((KV_HEADS, SHARE, TOK_DEV, 1), -jnp.inf, jnp.float32),
        jnp.zeros((KV_HEADS, SHARE, TOK_DEV, 1), jnp.float32),
    )
    out_start = jnp.zeros((TOK_DEV, KV_HEADS, SHARE, HEAD_DIM), jnp.float32)
    query_grad = jnp.zeros((TOK_DEV, KV_HEADS, SHARE, HEAD_DIM), jnp.float32)
    key_acc = jnp.zeros((TOK_DEV, KV_HEADS, HEAD_DIM), jnp.float32)
    value_acc = jnp.zeros((TOK_DEV, KV_HEADS, HEAD_DIM), jnp.float32)
    state_pair = stats_tile(start_state, key_pack, allowed[0])
    key_block = key_pack
    for offset in range(1, REACH + 1):
        key_block = shifted(key_block, "ctx", 1)
        state_pair = stats_tile(state_pair, key_block, allowed[offset])
    log_total = state_pair[0] + jnp.log(state_pair[1])
    out_sum = output_tile(out_start, key_pack, value_pack, allowed[0], log_total)
    key_block, value_block = (key_pack, value_pack)
    for offset in range(1, REACH + 1):
        key_block, value_block = shifted((key_block, value_block), "ctx", 1)
        out_sum = output_tile(out_sum, key_block, value_block, allowed[offset], log_total)
    row_delta = jnp.transpose(jnp.sum(grad_pack.astype(jnp.float32) * out_sum, axis=-1), (1, 2, 0))[
        ..., None
    ]
    key_block, value_block = (key_pack, value_pack)
    for offset in range(REACH + 1):
        if offset > 0:
            key_block, value_block = shifted((key_block, value_block), "ctx", 1)
            key_acc, value_acc = shifted_2((key_acc, value_acc), "ctx", 1)
        grad_tile_mask = allowed[offset]
        weights = jnp.where(grad_tile_mask, jnp.exp(scores_of(key_block) - log_total), 0.0)
        grad_weights_low = weights.astype(jnp.bfloat16)
        prob_grad = jnp.einsum(
            "ihgd,jhd->hgij", grad_pack, value_block, preferred_element_type=jnp.float32
        )
        score_grad = (weights * (prob_grad - row_delta)).astype(jnp.bfloat16)
        query_add = (
            jnp.einsum("hgij,jhd->ihgd", score_grad, key_block, preferred_element_type=jnp.float32)
            * score_scale
        )
        key_part = (
            jnp.einsum("hgij,ihgd->jhd", score_grad, query_pack, preferred_element_type=jnp.float32)
            * score_scale
        )
        value_part = jnp.einsum(
            "hgij,ihgd->jhd", grad_weights_low, grad_pack, preferred_element_type=jnp.float32
        )
        query_add, key_part, value_part = (query_add, key_part, value_part)
        query_grad = query_grad + query_add
        key_acc = key_acc + key_part
        value_acc = value_acc + value_part
    key_acc, value_acc = (
        shifted_2(key_acc.astype(jnp.bfloat16), "ctx", -REACH).astype(key_acc.dtype),
        shifted_2(value_acc.astype(jnp.bfloat16), "ctx", -REACH).astype(value_acc.dtype),
    )
    query_low = query_grad.astype(jnp.bfloat16).reshape(TOK_DEV, query_width)
    key_low = key_acc.astype(jnp.bfloat16).reshape(TOK_DEV, pair_width)
    value_low = value_acc.astype(jnp.bfloat16).reshape(TOK_DEV, pair_width)

    def back_slots(source):
        row_width = source.shape[-1]
        block_view = source.reshape(BLOCKS_DEV, BLOCK_ROWS * row_width)
        return apply_transposed(recv_table, block_view).reshape(
            members, capacity * BLOCK_ROWS, row_width
        )

    def back_blocks(source):
        row_width = source.shape[-1]
        block_view = source.reshape(members * capacity, BLOCK_ROWS * row_width)
        return apply_transposed(send_table, block_view).reshape(
            groups, per_group * BLOCK_ROWS, row_width
        )

    returned = (
        lax.all_to_all(back_slots(query_low), "ctx", split_axis=0, concat_axis=0, tiled=True),
        lax.all_to_all(back_slots(key_low), "ctx", split_axis=0, concat_axis=0, tiled=True),
        lax.all_to_all(back_slots(value_low), "ctx", split_axis=0, concat_axis=0, tiled=True),
    )
    returned_home = (
        lax.all_to_all(back_blocks(returned[0]), "grp", split_axis=0, concat_axis=0, tiled=True),
        lax.all_to_all(back_blocks(returned[1]), "grp", split_axis=0, concat_axis=0, tiled=True),
        lax.all_to_all(back_blocks(returned[2]), "grp", split_axis=0, concat_axis=0, tiled=True),
    )
    return (
        returned_home[0].reshape(TOK_DEV, query_width),
        returned_home[1].reshape(TOK_DEV, pair_width),
        returned_home[2].reshape(TOK_DEV, pair_width),
    )


def solution(mesh):
    in_specs = (
        P(("grp", "ctx"), None),
        P(("grp", "ctx"), None),
        P(("grp", "ctx"), None),
        P(("grp", "ctx"), None),
        P(),
        P("grp", None),
    )
    out_specs = (P(("grp", "ctx"), None), P(("grp", "ctx"), None), P(("grp", "ctx"), None))
    return jax.shard_map(
        on_device, mesh=mesh, in_specs=in_specs, out_specs=out_specs, check_vma=False
    )
```

profile of v0, /device:TPU:32, one launch (start us, length us, event | category | flops | bytes accessed | tf_op | source)
XLA Modules:
  0.0 496.9 jit_solution(5705076194595134632)
XLA Ops:
  0.6 5.5 %all-to-all-start = ((bf16[8,16,512]{2,1,0:T(8,128)(2,1)}), bf16[8,16,512]{2,1,0:T(8,128)(2,1)S(1)}, u32[]{:S(2)}, u32[]{:S(2)}) async-start(bf16[8,16,512]{2,1,0:T(8,128)(2,1)} %bitcast.431), calls=%async_computation | async-start | bytes 262144 | tf_op jit(solution)/shard_map/all_to_all | solution.py:96
  7.2 5.5 %all-to-all-done = bf16[8,16,512]{2,1,0:T(8,128)(2,1)S(1)} async-done(((bf16[8,16,512]{2,1,0:T(8,128)(2,1)}), bf16[8,16,512]{2,1,0:T(8,128)(2,1)S(1)}, u32[]{:S(2)}, u32[]{:S(2)}) %all-to-all-start) | async-done | bytes 131104 | tf_op jit(solution)/shard_map/all_to_all | solution.py:96
  12.7 3.4 all-to-all-start.4
  17.1 5.5 %all-to-all-done.4 = bf16[8,16,512]{2,1,0:T(8,128)(2,1)S(1)} async-done(((bf16[8,16,512]{2,1,0:T(8,128)(2,1)}), bf16[8,16,512]{2,1,0:T(8,128)(2,1)S(1)}, u32[]{:S(2)}, u32[]{:S(2)}) %all-to-all-start.4) | async-done | bytes 131104 | tf_op jit(solution)/shard_map/all_to_all | solution.py:103
  22.6 11.1 %all-to-all-start.1 = ((bf16[32,8,512]{2,1,0:T(8,128)(2,1)}), bf16[32,8,512]{2,1,0:T(8,128)(2,1)S(1)}, u32[]{:S(2)}, u32[]{:S(2)}) async-start(bf16[32,8,512]{2,1,0:T(8,128)(2,1)} %bitcast.102), calls=%async_computation.1 | async-start | bytes 524288 | tf_op jit(solution)/shard_map/all_to_all | solution.py:134
  34.0 13.3 %all-to-all-done.1 = bf16[32,8,512]{2,1,0:T(8,128)(2,1)S(1)} async-done(((bf16[32,8,512]{2,1,0:T(8,128)(2,1)}), bf16[32,8,512]{2,1,0:T(8,128)(2,1)S(1)}, u32[]{:S(2)}, u32[]{:S(2)}) %all-to-all-start.1) | async-done | bytes 262176 | tf_op jit(solution)/shard_map/all_to_all | solution.py:134
  47.3 18.3 %all_to_all.70 = bf16[32,8,512]{2,1,0:T(8,128)(2,1)} all-to-all(bf16[32,8,512]{2,1,0:T(8,128)(2,1)S(1)} %bitcast.416), channel_id=1, replica_groups=mesh['grp'=8,'ctx'=32] {'ctx'}, dimensions={0} | all-to-all | bytes 524288 | tf_op jit(solution)/shard_map/all_to_all | solution.py:135
  65.6 17.6 %all_to_all.71 = bf16[8,16,4096]{2,1,0:T(8,128)(2,1)S(1)} all-to-all(bf16[8,16,4096]{2,1,0:T(8,128)(2,1)S(1)} %bitcast.410), channel_id=1, replica_groups=mesh['grp'=8,'ctx'=32] {'grp'}, dimensions={0} | all-to-all | bytes 2097152 | tf_op jit(solution)/shard_map/all_to_all | solution.py:89
  83.2 3.6 all-to-all-start.6
  90.6 10.7 %all-to-all-done.6 = bf16[8,16,4096]{2,1,0:T(8,128)(2,1)S(1)} async-done(((bf16[8,16,4096]{2,1,0:T(8,128)(2,1)}), bf16[8,16,4096]{2,1,0:T(8,128)(2,1)S(1)}, u32[]{:S(2)}, u32[]{:S(2)}) %all-to-all-start.6) | async-done | bytes 1048608 | tf_op jit(solution)/shard_map/all_to_all | solution.py:110
  101.2 5.8 %all-to-all-start.3 = ((bf16[32,8,4096]{2,1,0:T(8,128)(2,1)}), bf16[32,8,4096]{2,1,0:T(8,128)(2,1)S(1)}, u32[]{:S(2)}, u32[]{:S(2)}) async-start(bf16[32,8,4096]{2,1,0:T(8,128)(2,1)} %bitcast.397), calls=%async_computation.3 | async-start | bytes 4194304 | tf_op jit(solution)/shard_map/all_to_all | solution.py:133
  112.8 3.3 collective-permute-start.4
  117.7 37.4 %collective-permute-done = bf16[128,4,128]{2,0,1:T(8,128)(2,1)} collective-permute-done((bf16[128,4,128]{2,0,1:T(8,128)(2,1)}, bf16[128,4,128]{2,0,1:T(8,128)(2,1)}, u32[]{:S(2)}, u32[]{:S(2)}) %collective-permute-start) | collective-permute-done | bytes 131104 | tf_op jit(solution)/shard_map/ppermute | solution.py:18
  157.0 3.5 collective-permute-start.5
  164.4 3.3 collective-permute-start.6
  175.4 4.7 collective-permute-start.7
  180.1 10.6 %all-to-all-start.7 = ((bf16[32,8,4096]{2,1,0:T(8,128)(2,1)}), bf16[32,8,4096]{2,1,0:T(8,128)(2,1)}, u32[]{:S(2)}, u32[]{:S(2)}) async-start(bf16[32,8,4096]{2,1,0:T(8,128)(2,1)} %bitcast.398), calls=%async_computation.7 | async-start | bytes 4194304 | tf_op jit(solution)/shard_map/all_to_all | solution.py:136
  200.9 3.5 fusion.45
  207.1 36.4 %all-to-all-done.7 = bf16[32,8,4096]{2,1,0:T(8,128)(2,1)} async-done(((bf16[32,8,4096]{2,1,0:T(8,128)(2,1)}), bf16[32,8,4096]{2,1,0:T(8,128)(2,1)}, u32[]{:S(2)}, u32[]{:S(2)}) %all-to-all-start.7) | async-done | bytes 2097184 | tf_op jit(solution)/shard_map/all_to_all | solution.py:136
  281.6 4.4 fusion.8
  336.3 11.9 %collective-permute-start.17 = (bf16[128,4,128]{0,2,1:T(8,128)(2,1)S(1)}, bf16[128,4,128]{0,2,1:T(8,128)(2,1)S(1)}, u32[]{:S(2)}, u32[]{:S(2)}) collective-permute-start(bf16[128,4,128]{0,2,1:T(8,128)(2,1)S(1)} %add_convert_fusion), channel_id=1, source_target_pairs={{4,0},{5,1},{6,2},{7,3},{8,4},{9,5},{10,6},{11,7},{12,8},{13,9},{1... | collective-permute-start | bytes 393224 | tf_op jit(solution)/shard_map/ppermute | solution.py:24
  351.9 14.6 %all-to-all-start.12 = ((bf16[32,8,512]{2,1,0:T(8,128)(2,1)}), bf16[32,8,512]{2,1,0:T(8,128)(2,1)S(1)}, u32[]{:S(2)}, u32[]{:S(2)}) async-start(bf16[32,8,512]{2,1,0:T(8,128)(2,1)} %bitcast.127), calls=%async_computation.12 | async-start | bytes 524288 | tf_op jit(solution)/shard_map/all_to_all | solution.py:248
  369.7 10.4 %all-to-all-done.12 = bf16[32,8,512]{2,1,0:T(8,128)(2,1)S(1)} async-done(((bf16[32,8,512]{2,1,0:T(8,128)(2,1)}), bf16[32,8,512]{2,1,0:T(8,128)(2,1)S(1)}, u32[]{:S(2)}, u32[]{:S(2)}) %all-to-all-start.12) | async-done | bytes 262176 | tf_op jit(solution)/shard_map/all_to_all | solution.py:248
  380.2 5.5 %all-to-all-start.10 = ((bf16[32,8,512]{2,1,0:T(8,128)(2,1)}), bf16[32,8,512]{2,1,0:T(8,128)(2,1)}, u32[]{:S(2)}, u32[]{:S(2)}) async-start(bf16[32,8,512]{2,1,0:T(8,128)(2,1)} %bitcast.123), calls=%async_computation.10 | async-start | bytes 524288 | tf_op jit(solution)/shard_map/all_to_all | solution.py:247
  385.6 4.2 fusion.46
  394.6 4.8 all-to-all-done.10
  399.4 5.2 %all-to-all-start.8 = ((bf16[32,8,4096]{2,1,0:T(8,128)(2,1)}), bf16[32,8,4096]{2,1,0:T(8,128)(2,1)S(1)}, u32[]{:S(2)}, u32[]{:S(2)}) async-start(bf16[32,8,4096]{2,1,0:T(8,128)(2,1)} %bitcast.400), calls=%async_computation.8 | async-start | bytes 4194304 | tf_op jit(solution)/shard_map/all_to_all | solution.py:246
  406.7 50.9 %all-to-all-done.8 = bf16[32,8,4096]{2,1,0:T(8,128)(2,1)S(1)} async-done(((bf16[32,8,4096]{2,1,0:T(8,128)(2,1)}), bf16[32,8,4096]{2,1,0:T(8,128)(2,1)S(1)}, u32[]{:S(2)}, u32[]{:S(2)}) %all-to-all-start.8) | async-done | bytes 2097184 | tf_op jit(solution)/shard_map/all_to_all | solution.py:246
  457.6 3.4 all-to-all-start.13
  467.5 3.4 all-to-all-start.11
  477.4 3.6 all-to-all-start.9
  481.0 13.4 %all-to-all-done.9 = bf16[8,16,4096]{2,1,0:T(8,128)(2,1)S(1)} async-done(((bf16[8,16,4096]{2,1,0:T(8,128)(2,1)}), bf16[8,16,4096]{2,1,0:T(8,128)(2,1)S(1)}, u32[]{:S(2)}, u32[]{:S(2)}) %all-to-all-start.9) | async-done | bytes 1048608 | tf_op jit(solution)/shard_map/all_to_all | solution.py:251
  (248 shorter events, 156.5 us)
Async XLA Ops:
  0.6 65.0 %copy-start.20 = (bf16[128,4096]{1,0:T(8,128)(2,1)S(1)}, bf16[128,4096]{1,0:T(8,128)(2,1)}, u32[]{:S(2)}) copy-start(bf16[128,4096]{1,0:T(8,128)(2,1)} %param.6) | copy-start | bytes 3145732
  0.6 12.0 %all-to-all-start = ((bf16[8,16,512]{2,1,0:T(8,128)(2,1)}), bf16[8,16,512]{2,1,0:T(8,128)(2,1)S(1)}, u32[]{:S(2)}, u32[]{:S(2)}) async-start(bf16[8,16,512]{2,1,0:T(8,128)(2,1)} %bitcast.431), calls=%async_computation | async-start | bytes 262144 | tf_op jit(solution)/shard_map/all_to_all | solution.py:96
  7.2 80.2 %copy-start.44 = (s32[16]{0:T(128)}, s32[16]{0:T(128)S(1)}, u32[]{:S(2)}) copy-start(s32[16]{0:T(128)S(1)} %add_reduce_fusion) | copy-start | bytes 196
  12.7 9.9 %all-to-all-start.4 = ((bf16[8,16,512]{2,1,0:T(8,128)(2,1)}), bf16[8,16,512]{2,1,0:T(8,128)(2,1)S(1)}, u32[]{:S(2)}, u32[]{:S(2)}) async-start(bf16[8,16,512]{2,1,0:T(8,128)(2,1)} %bitcast.432), calls=%async_computation.4 | async-start | bytes 262144 | tf_op jit(solution)/shard_map/all_to_all | solution.py:103
  22.6 24.7 %all-to-all-start.1 = ((bf16[32,8,512]{2,1,0:T(8,128)(2,1)}), bf16[32,8,512]{2,1,0:T(8,128)(2,1)S(1)}, u32[]{:S(2)}, u32[]{:S(2)}) async-start(bf16[32,8,512]{2,1,0:T(8,128)(2,1)} %bitcast.102), calls=%async_computation.1 | async-start | bytes 524288 | tf_op jit(solution)/shard_map/all_to_all | solution.py:134
  83.2 18.0 %all-to-all-start.6 = ((bf16[8,16,4096]{2,1,0:T(8,128)(2,1)}), bf16[8,16,4096]{2,1,0:T(8,128)(2,1)S(1)}, u32[]{:S(2)}, u32[]{:S(2)}) async-start(bf16[8,16,4096]{2,1,0:T(8,128)(2,1)} %bitcast.411), calls=%async_computation.6 | async-start | bytes 2097152 | tf_op jit(solution)/shard_map/all_to_all | solution.py:110
  101.2 78.8 %all-to-all-start.3 = ((bf16[32,8,4096]{2,1,0:T(8,128)(2,1)}), bf16[32,8,4096]{2,1,0:T(8,128)(2,1)S(1)}, u32[]{:S(2)}, u32[]{:S(2)}) async-start(bf16[32,8,4096]{2,1,0:T(8,128)(2,1)} %bitcast.397), calls=%async_computation.3 | async-start | bytes 4194304 | tf_op jit(solution)/shard_map/all_to_all | solution.py:133
  109.3 45.8 %collective-permute-start = (bf16[128,4,128]{2,0,1:T(8,128)(2,1)}, bf16[128,4,128]{2,0,1:T(8,128)(2,1)}, u32[]{:S(2)}, u32[]{:S(2)}) collective-permute-start(bf16[128,4,128]{2,0,1:T(8,128)(2,1)} %copy.184), channel_id=1, source_target_pairs={{0,1},{1,2},{2,3},{3,4},{4,5},{5,6},{6,7},{7,8},{8,9},{9,10},{10,1... | collective-permute-start | bytes 393224 | tf_op jit(solution)/shard_map/ppermute | solution.py:18
  112.8 44.2 %collective-permute-start.4 = (bf16[128,4,128]{0,2,1:T(8,128)(2,1)S(1)}, bf16[128,4,128]{0,2,1:T(8,128)(2,1)}, u32[]{:S(2)}, u32[]{:S(2)}) collective-permute-start(bf16[128,4,128]{0,2,1:T(8,128)(2,1)S(1)} %copy.194), channel_id=1, source_target_pairs={{0,1},{1,2},{2,3},{3,4},{4,5},{5,6},{6,7},{7,8},{8,9},{9,10},{10,1... | collective-permute-start | bytes 393224 | tf_op jit(solution)/shard_map/ppermute | solution.py:18
  155.1 7.4 %collective-permute-start.1 = (bf16[128,4,128]{2,0,1:T(8,128)(2,1)}, bf16[128,4,128]{2,0,1:T(8,128)(2,1)}, u32[]{:S(2)}, u32[]{:S(2)}) collective-permute-start(bf16[128,4,128]{2,0,1:T(8,128)(2,1)} %collective-permute-done), channel_id=1, source_target_pairs={{0,1},{1,2},{2,3},{3,4},{4,5},{5,6},{6,7},{7,8},{8,9},{9,10},{10,1... | collective-permute-start | bytes 393224 | tf_op jit(solution)/shard_map/ppermute | solution.py:18
  157.0 7.4 %collective-permute-start.5 = (bf16[128,4,128]{0,2,1:T(8,128)(2,1)}, bf16[128,4,128]{0,2,1:T(8,128)(2,1)}, u32[]{:S(2)}, u32[]{:S(2)}) collective-permute-start(bf16[128,4,128]{0,2,1:T(8,128)(2,1)} %collective-permute-done.4), channel_id=1, source_target_pairs={{0,1},{1,2},{2,3},{3,4},{4,5},{5,6},{6,7},{7,8},{8,9},{9,10},{10,1... | collective-permute-start | bytes 393224 | tf_op jit(solution)/shard_map/ppermute | solution.py:18
  162.4 11.0 %collective-permute-start.2 = (bf16[128,4,128]{2,0,1:T(8,128)(2,1)}, bf16[128,4,128]{2,0,1:T(8,128)(2,1)S(1)}, u32[]{:S(2)}, u32[]{:S(2)}) collective-permute-start(bf16[128,4,128]{2,0,1:T(8,128)(2,1)} %collective-permute-done.1), channel_id=1, source_target_pairs={{0,1},{1,2},{2,3},{3,4},{4,5},{5,6},{6,7},{7,8},{8,9},{9,10},{10,1... | collective-permute-start | bytes 393224 | tf_op jit(solution)/shard_map/ppermute | solution.py:18
  164.4 11.0 %collective-permute-start.6 = (bf16[128,4,128]{0,2,1:T(8,128)(2,1)}, bf16[128,4,128]{0,2,1:T(8,128)(2,1)}, u32[]{:S(2)}, u32[]{:S(2)}) collective-permute-start(bf16[128,4,128]{0,2,1:T(8,128)(2,1)} %collective-permute-done.5), channel_id=1, source_target_pairs={{0,1},{1,2},{2,3},{3,4},{4,5},{5,6},{6,7},{7,8},{8,9},{9,10},{10,1... | collective-permute-start | bytes 393224 | tf_op jit(solution)/shard_map/ppermute | solution.py:18
  173.5 24.3 %collective-permute-start.3 = (bf16[128,4,128]{2,0,1:T(8,128)(2,1)S(1)}, bf16[128,4,128]{2,0,1:T(8,128)(2,1)S(1)}, u32[]{:S(2)}, u32[]{:S(2)}) collective-permute-start(bf16[128,4,128]{2,0,1:T(8,128)(2,1)S(1)} %collective-permute-done.2), channel_id=1, source_target_pairs={{0,1},{1,2},{2,3},{3,4},{4,5},{5,6},{6,7},{7,8},{8,9},{9,10},{10,1... | collective-permute-start | bytes 393224 | tf_op jit(solution)/shard_map/ppermute | solution.py:18
  175.4 106.2 %collective-permute-start.7 = (bf16[128,4,128]{0,2,1:T(8,128)(2,1)}, bf16[128,4,128]{0,2,1:T(8,128)(2,1)}, u32[]{:S(2)}, u32[]{:S(2)}) collective-permute-start(bf16[128,4,128]{0,2,1:T(8,128)(2,1)} %collective-permute-done.6), channel_id=1, source_target_pairs={{0,1},{1,2},{2,3},{3,4},{4,5},{5,6},{6,7},{7,8},{8,9},{9,10},{10,1... | collective-permute-start | bytes 393224 | tf_op jit(solution)/shard_map/ppermute | solution.py:18
  180.1 63.4 %all-to-all-start.7 = ((bf16[32,8,4096]{2,1,0:T(8,128)(2,1)}), bf16[32,8,4096]{2,1,0:T(8,128)(2,1)}, u32[]{:S(2)}, u32[]{:S(2)}) async-start(bf16[32,8,4096]{2,1,0:T(8,128)(2,1)} %bitcast.398), calls=%async_computation.7 | async-start | bytes 4194304 | tf_op jit(solution)/shard_map/all_to_all | solution.py:136
  252.7 63.9 %collective-permute-start.13 = (f32[128,4,128]{0,2,1:T(8,128)}, f32[128,4,128]{0,2,1:T(8,128)}, u32[]{:S(2)}, u32[]{:S(2)}) collective-permute-start(f32[128,4,128]{0,2,1:T(8,128)} %convolution_bitcast_fusion.4), channel_id=1, source_target_pairs={{31,0},{0,1},{1,2},{2,3},{3,4},{4,5},{5,6},{6,7},{7,8},{8,9},{9,10... | collective-permute-start | bytes 786440 | tf_op jit(solution)/shard_map/ppermute | solution.py:24
  291.0 27.6 %collective-permute-start.8 = (f32[128,4,128]{0,2,1:T(8,128)}, f32[128,4,128]{0,2,1:T(8,128)}, u32[]{:S(2)}, u32[]{:S(2)}) collective-permute-start(f32[128,4,128]{0,2,1:T(8,128)} %fusion.56), channel_id=1, source_target_pairs={{31,0},{0,1},{1,2},{2,3},{3,4},{4,5},{5,6},{6,7},{7,8},{8,9},{9,10... | collective-permute-start | bytes 786440 | tf_op jit(solution)/shard_map/ppermute | solution.py:24
  318.5 5.9 %collective-permute-start.14 = (f32[128,4,128]{0,2,1:T(8,128)S(1)}, f32[128,4,128]{0,2,1:T(8,128)S(1)}, u32[]{:S(2)}, u32[]{:S(2)}) collective-permute-start(f32[128,4,128]{0,2,1:T(8,128)S(1)} %fusion.58), channel_id=1, source_target_pairs={{31,0},{0,1},{1,2},{2,3},{3,4},{4,5},{5,6},{6,7},{7,8},{8,9},{9,10... | collective-permute-start | bytes 786440 | tf_op jit(solution)/shard_map/ppermute | solution.py:24
  320.1 7.0 %collective-permute-start.9 = (f32[128,4,128]{0,2,1:T(8,128)S(1)}, f32[128,4,128]{0,2,1:T(8,128)S(1)}, u32[]{:S(2)}, u32[]{:S(2)}) collective-permute-start(f32[128,4,128]{0,2,1:T(8,128)S(1)} %fusion.57), channel_id=1, source_target_pairs={{31,0},{0,1},{1,2},{2,3},{3,4},{4,5},{5,6},{6,7},{7,8},{8,9},{9,10... | collective-permute-start | bytes 786440 | tf_op jit(solution)/shard_map/ppermute | solution.py:24
  324.4 5.9 %collective-permute-start.15 = (f32[128,4,128]{0,2,1:T(8,128)S(1)}, f32[128,4,128]{0,2,1:T(8,128)S(1)}, u32[]{:S(2)}, u32[]{:S(2)}) collective-permute-start(f32[128,4,128]{0,2,1:T(8,128)S(1)} %add.253), channel_id=1, source_target_pairs={{31,0},{0,1},{1,2},{2,3},{3,4},{4,5},{5,6},{6,7},{7,8},{8,9},{9,10... | collective-permute-start | bytes 786440 | tf_op jit(solution)/shard_map/ppermute | solution.py:24
  327.2 5.9 %collective-permute-start.10 = (f32[128,4,128]{0,2,1:T(8,128)S(1)}, f32[128,4,128]{0,2,1:T(8,128)S(1)}, u32[]{:S(2)}, u32[]{:S(2)}) collective-permute-start(f32[128,4,128]{0,2,1:T(8,128)S(1)} %add.249), channel_id=1, source_target_pairs={{31,0},{0,1},{1,2},{2,3},{3,4},{4,5},{5,6},{6,7},{7,8},{8,9},{9,10... | collective-permute-start | bytes 786440 | tf_op jit(solution)/shard_map/ppermute | solution.py:24
  330.3 5.9 %collective-permute-start.16 = (f32[128,4,128]{0,2,1:T(8,128)S(1)}, f32[128,4,128]{0,2,1:T(8,128)S(1)}, u32[]{:S(2)}, u32[]{:S(2)}) collective-permute-start(f32[128,4,128]{0,2,1:T(8,128)S(1)} %add.254), channel_id=1, source_target_pairs={{31,0},{0,1},{1,2},{2,3},{3,4},{4,5},{5,6},{6,7},{7,8},{8,9},{9,10... | collective-permute-start | bytes 786440 | tf_op jit(solution)/shard_map/ppermute | solution.py:24
  333.2 15.0 %collective-permute-start.11 = (f32[128,4,128]{0,2,1:T(8,128)S(1)}, f32[128,4,128]{0,2,1:T(8,128)S(1)}, u32[]{:S(2)}, u32[]{:S(2)}) collective-permute-start(f32[128,4,128]{0,2,1:T(8,128)S(1)} %add.250), channel_id=1, source_target_pairs={{31,0},{0,1},{1,2},{2,3},{3,4},{4,5},{5,6},{6,7},{7,8},{8,9},{9,10... | collective-permute-start | bytes 786440 | tf_op jit(solution)/shard_map/ppermute | solution.py:24
  336.3 14.4 %collective-permute-start.17 = (bf16[128,4,128]{0,2,1:T(8,128)(2,1)S(1)}, bf16[128,4,128]{0,2,1:T(8,128)(2,1)S(1)}, u32[]{:S(2)}, u32[]{:S(2)}) collective-permute-start(bf16[128,4,128]{0,2,1:T(8,128)(2,1)S(1)} %add_convert_fusion), channel_id=1, source_target_pairs={{4,0},{5,1},{6,2},{7,3},{8,4},{9,5},{10,6},{11,7},{12,8},{13,9},{1... | collective-permute-start | bytes 393224 | tf_op jit(solution)/shard_map/ppermute | solution.py:24
  348.2 20.3 %collective-permute-start.12 = (bf16[128,4,128]{0,2,1:T(8,128)(2,1)S(1)}, bf16[128,4,128]{0,2,1:T(8,128)(2,1)S(1)}, u32[]{:S(2)}, u32[]{:S(2)}) collective-permute-start(bf16[128,4,128]{0,2,1:T(8,128)(2,1)S(1)} %add_convert_fusion.1), channel_id=1, source_target_pairs={{4,0},{5,1},{6,2},{7,3},{8,4},{9,5},{10,6},{11,7},{12,8},{13,9},{1... | collective-permute-start | bytes 393224 | tf_op jit(solution)/shard_map/ppermute | solution.py:24
  351.9 28.2 %all-to-all-start.12 = ((bf16[32,8,512]{2,1,0:T(8,128)(2,1)}), bf16[32,8,512]{2,1,0:T(8,128)(2,1)S(1)}, u32[]{:S(2)}, u32[]{:S(2)}) async-start(bf16[32,8,512]{2,1,0:T(8,128)(2,1)} %bitcast.127), calls=%async_computation.12 | async-start | bytes 524288 | tf_op jit(solution)/shard_map/all_to_all | solution.py:248
  380.2 19.3 %all-to-all-start.10 = ((bf16[32,8,512]{2,1,0:T(8,128)(2,1)}), bf16[32,8,512]{2,1,0:T(8,128)(2,1)}, u32[]{:S(2)}, u32[]{:S(2)}) async-start(bf16[32,8,512]{2,1,0:T(8,128)(2,1)} %bitcast.123), calls=%async_computation.10 | async-start | bytes 524288 | tf_op jit(solution)/shard_map/all_to_all | solution.py:247
  399.4 58.2 %all-to-all-start.8 = ((bf16[32,8,4096]{2,1,0:T(8,128)(2,1)}), bf16[32,8,4096]{2,1,0:T(8,128)(2,1)S(1)}, u32[]{:S(2)}, u32[]{:S(2)}) async-start(bf16[32,8,4096]{2,1,0:T(8,128)(2,1)} %bitcast.400), calls=%async_computation.8 | async-start | bytes 4194304 | tf_op jit(solution)/shard_map/all_to_all | solution.py:246
  457.6 9.9 %all-to-all-start.13 = ((bf16[8,16,512]{2,1,0:T(8,128)(2,1)}), bf16[8,16,512]{2,1,0:T(8,128)(2,1)S(1)}, u32[]{:S(2)}, u32[]{:S(2)}) async-start(bf16[8,16,512]{2,1,0:T(8,128)(2,1)} %reshape.421), calls=%async_computation.13 | async-start | bytes 262144 | tf_op jit(solution)/shard_map/all_to_all | solution.py:253
  467.5 9.9 %all-to-all-start.11 = ((bf16[8,16,512]{2,1,0:T(8,128)(2,1)}), bf16[8,16,512]{2,1,0:T(8,128)(2,1)S(1)}, u32[]{:S(2)}, u32[]{:S(2)}) async-start(bf16[8,16,512]{2,1,0:T(8,128)(2,1)} %reshape.417), calls=%async_computation.11 | async-start | bytes 262144 | tf_op jit(solution)/shard_map/all_to_all | solution.py:252
  477.4 17.0 %all-to-all-start.9 = ((bf16[8,16,4096]{2,1,0:T(8,128)(2,1)}), bf16[8,16,4096]{2,1,0:T(8,128)(2,1)S(1)}, u32[]{:S(2)}, u32[]{:S(2)}) async-start(bf16[8,16,4096]{2,1,0:T(8,128)(2,1)} %reshape.413), calls=%async_computation.9 | async-start | bytes 2097152 | tf_op jit(solution)/shard_map/all_to_all | solution.py:251
  (45 other events, 260.2 us)
where the time goes:
time: 506 us; the launch traced here: 497 us
  waiting for transfers between devices  205 us (41%)
  starting transfers between devices  111 us (22%)
  matrix products  75.8 us (15%)
  local copies, waits for them, and re-layouts  55.8 us (11%)
  blocking collectives  35.9 us (7%)
  other arithmetic  11.3 us (2%)
    all_to_all x1, waiting for transfers between devices, on_device(): lax.all_to_all(back_slots(query_low), 'ctx', split_axis=0, concat_axis=0,...  50.9 us
    ppermute x8, waiting for transfers between devices, shifted(): return lax.ppermute(shard, axis, pairs)  37.4 us
    all_to_all x1, waiting for transfers between devices, on_device(): lax.all_to_all(to_slots(arrived[3]), 'ctx', split_axis=0, concat_axis=0,...  36.4 us
    ppermute x8, starting transfers between devices, shifted(): return lax.ppermute(shard, axis, pairs)  22.7 us
    unnamed x111, local copies, waits for them, and re-layouts  21.2 us
    all_to_all x1, blocking collectives, on_device(): lax.all_to_all(to_slots(arrived[2]), 'ctx', split_axis=0, concat_axis=0,...  18.3 us
    all_to_all x1, blocking collectives, on_device(): lax.all_to_all(query_rows.reshape(groups, per_group * BLOCK_ROWS, query_w...  17.6 us
    all_to_all x1, starting transfers between devices, on_device(): lax.all_to_all(back_slots(value_low), 'ctx', split_axis=0, concat_axis=0,...  14.6 us
  transfers between devices with their start and end apart: 30, of which 17 were waited for; matrix products, arithmetic and copies ran while one was open for 28% of the time, Pallas kernels for 0%

commit v1 on v0

v1 whole, which is shorter than its diff:
```python
import jax
import jax.numpy as jnp
from jax import lax
from jax.experimental import pallas as pl
from jax.experimental.pallas import tpu as pltpu
from jax.sharding import PartitionSpec as P

KV_HEADS = 4
HEAD_DIM = 128
SHARE = 8
BLOCK_ROWS = 8
GROUPS = 8
PLANES = 8
PEERS = 32
RUN = 16
UNIT = SHARE * HEAD_DIM
GROUP_BLOCKS = 512
GROUP_TOKENS = 4096
PLANE_BLOCKS = 64
DOCS = 16
TILE_BLOCKS = 4
TILE_ROWS = TILE_BLOCKS * SHARE * BLOCK_ROWS
TILES = PLANE_BLOCKS // TILE_BLOCKS
KEY_TILE = 256
KEY_TILES = GROUP_TOKENS // KEY_TILE
SCORE_SCALE = HEAD_DIM**-0.5
EXP2_SCALE = SCORE_SCALE * 1.4426950408889634
MESH = pl.DeviceIdType.MESH
F32 = jnp.float32
BF16 = jnp.bfloat16


def place():
    group = lax.axis_index("grp")
    ctx = lax.axis_index("ctx")
    y_hi = ctx // 16
    plane = (ctx // 2) % PLANES
    core = ctx % 2
    head = y_hi * 2 + core
    return group, head, plane


def device_of(group, head, plane):
    return {"grp": group, "ctx": (head // 2) * 16 + plane * 2 + head % 2}


def greet(group, head, plane):
    barrier = pltpu.get_barrier_semaphore()
    me = group * KV_HEADS + head

    def one(step, carry):
        peer = lax.rem(me + step, PEERS)
        pl.semaphore_signal(
            barrier,
            inc=1,
            device_id=device_of(peer // KV_HEADS, lax.rem(peer, KV_HEADS), plane),
            device_id_type=MESH,
        )
        return carry

    lax.fori_loop(1, PEERS, one, 0)
    for by in (1, PLANES - 1):
        pl.semaphore_signal(
            barrier,
            inc=1,
            device_id=device_of(group, head, lax.rem(plane + by, PLANES)),
            device_id_type=MESH,
        )
    pl.semaphore_wait(barrier, PEERS - 1 + 2)


def remote(src, dst, send, recv, device):
    return pltpu.make_async_remote_copy(
        src_ref=src, dst_ref=dst, send_sem=send, recv_sem=recv, device_id=device, device_id_type=MESH
    )


def scatter_kernel(
    q_ref, g_ref, k_ref, v_ref, q_out, g_out, k_out, v_out, in_send, in_recv, own_sem, ring_send, ring_recv
):
    group, head, plane = place()
    me = group * KV_HEADS + head
    greet(group, head, plane)
    narrow = ((k_ref, k_out), (v_ref, v_out))
    wide = ((q_ref, q_out), (g_ref, g_out))

    def run_of(ref, to_group, to_head, width):
        return ref.at[
            pl.ds(pl.multiple_of(to_group * RUN, RUN), RUN),
            pl.ds(pl.multiple_of(to_head * width, width), width),
        ]

    def send_narrow(step, carry):
        peer = lax.rem(me + step, PEERS)
        to_group, to_head = peer // KV_HEADS, lax.rem(peer, KV_HEADS)
        for n, (src, dst) in enumerate(narrow):
            remote(
                run_of(src, to_group, to_head, HEAD_DIM),
                dst.at[plane, me],
                in_send.at[n],
                in_recv.at[n],
                device_of(to_group, to_head, plane),
            ).start()
        return carry

    def send_wide(step, carry):
        peer = lax.rem(me + step, PEERS)
        to_group, to_head = peer // KV_HEADS, lax.rem(peer, KV_HEADS)
        for n, (src, dst) in enumerate(wide):
            remote(
                run_of(src, to_group, to_head, UNIT),
                dst.at[me],
                in_send.at[2 + n],
                in_recv.at[2 + n],
                device_of(to_group, to_head, plane),
            ).start()
        return carry

    lax.fori_loop(1, PEERS, send_narrow, 0)
    own = [
        pltpu.make_async_copy(run_of(src, group, head, HEAD_DIM), dst.at[plane, me], own_sem.at[n])
        for n, (src, dst) in enumerate(narrow)
    ] + [
        pltpu.make_async_copy(run_of(src, group, head, UNIT), dst.at[me], own_sem.at[2 + n])
        for n, (src, dst) in enumerate(wide)
    ]
    for copy in own:
        copy.start()
    lax.fori_loop(1, PEERS, send_wide, 0)

    here = device_of(group, head, plane)
    rest_narrow = [
        remote(dst.at[0, pl.ds(0, PEERS - 1)], dst.at[0, pl.ds(0, PEERS - 1)], in_send.at[n], in_recv.at[n], here)
        for n, (_, dst) in enumerate(narrow)
    ]
    rest_wide = [
        remote(dst.at[pl.ds(0, PEERS - 1)], dst.at[pl.ds(0, PEERS - 1)], in_send.at[2 + n], in_recv.at[2 + n], here)
        for n, (_, dst) in enumerate(wide)
    ]
    for n in range(2):
        own[n].wait()
        rest_narrow[n].wait_recv()

    def ring(way, step, n):
        chunk = lax.rem(plane + (PLANES - step if way == 0 else step), PLANES)
        target = lax.rem(plane + (1 if way == 0 else PLANES - 1), PLANES)
        out = narrow[n][1]
        return remote(
            out.at[chunk],
            out.at[chunk],
            ring_send.at[way, step, n],
            ring_recv.at[way, step, n],
            device_of(group, head, target),
        )

    started = []
    for step in range(4):
        for way in range(2):
            for n in range(2):
                if step == 3 and n != way:
                    continue
                if step > 0:
                    ring(way, step - 1, n).wait_recv()
                copy = ring(way, step, n)
                copy.start()
                started.append(copy)
    for way in range(2):
        ring(way, 3, way).wait_recv()
        ring(way, 2, 1 - way).wait_recv()
    for copy in started:
        copy.wait_send()
    for n in range(2):
        rest_narrow[n].wait_send()
        own[2 + n].wait()
        rest_wide[n].wait_recv()
        rest_wide[n].wait_send()


def scatter(query_rows, output_grad, key_rows, value_rows):
    wide = jax.ShapeDtypeStruct((PEERS, RUN, UNIT), BF16)
    narrow = jax.ShapeDtypeStruct((PLANES, PEERS, RUN, HEAD_DIM), BF16)
    return pl.pallas_call(
        scatter_kernel,
        name="scatter",
        out_shape=(wide, wide, narrow, narrow),
        in_specs=[pl.BlockSpec(memory_space=pl.ANY)] * 4,
        out_specs=[pl.BlockSpec(memory_space=pl.ANY)] * 4,
        scratch_shapes=[
            pltpu.SemaphoreType.DMA((4,)),
            pltpu.SemaphoreType.DMA((4,)),
            pltpu.SemaphoreType.DMA((4,)),
            pltpu.SemaphoreType.DMA((2, 4, 2)),
            pltpu.SemaphoreType.DMA((2, 4, 2)),
        ],
        compiler_params=pltpu.CompilerParams(collective_id=0, has_side_effects=True),
    )(query_rows, output_grad, key_rows, value_rows)


def attention_kernel(
    packed_from,
    packed_to,
    query_order,
    query_block,
    doc_ends,
    q_ref,
    g_ref,
    k_ref,
    v_ref,
    dq_ref,
    dk_ref,
    dv_ref,
    k_pack,
    v_pack,
    k_turned,
    dk_acc,
    dv_acc,
    dq_acc,
    exps,
    probs,
    maxes,
):
    def half_of(pair, which):
        wide = pair.astype(F32)
        return jnp.where(which == 0, wide[:BLOCK_ROWS], wide[BLOCK_ROWS:])

    def gather(step, carry):
        first = packed_from[2 * step]
        second = packed_from[2 * step + 1]
        for src, dst in ((k_ref, k_pack), (v_ref, v_pack)):
            rows = jnp.concatenate(
                [half_of(src[first >> 1], first & 1), half_of(src[second >> 1], second & 1)], axis=0
            )
            dst[pl.ds(pl.multiple_of(step * RUN, RUN), RUN), :] = rows.astype(BF16)
        return carry

    lax.fori_loop(0, GROUP_BLOCKS // 2, gather, 0, unroll=8)

    def turn(step, carry):
        rows = pl.ds(pl.multiple_of(step * KEY_TILE, KEY_TILE), KEY_TILE)
        k_turned[step] = jnp.transpose(k_pack[rows, :].astype(F32)).astype(BF16)
        dk_acc[rows, :] = jnp.zeros((KEY_TILE, HEAD_DIM), F32)
        dv_acc[rows, :] = jnp.zeros((KEY_TILE, HEAD_DIM), F32)
        return carry

    lax.fori_loop(0, KEY_TILES, turn, 0)

    lane = lax.broadcasted_iota(jnp.int32, (1, TILE_ROWS), 1)
    key_iota = lax.broadcasted_iota(jnp.int32, (KEY_TILE, TILE_ROWS), 0)

    def query_tile(tile, carry):
        slots = [query_order[tile * TILE_BLOCKS + n] for n in range(TILE_BLOCKS)]
        blocks = [query_block[tile * TILE_BLOCKS + n] for n in range(TILE_BLOCKS)]

        def stacked(ref):
            parts = []
            for slot in slots:
                rows = half_of(ref[slot >> 1], slot & 1)
                parts += [rows[:, h * HEAD_DIM : (h + 1) * HEAD_DIM] for h in range(SHARE)]
            return jnp.concatenate(parts, axis=0)

        queries = stacked(q_ref)
        grads = stacked(g_ref)
        q_low, g_low = queries.astype(BF16), grads.astype(BF16)
        q_turned = jnp.transpose(queries).astype(BF16)
        g_turned = jnp.transpose(grads).astype(BF16)

        owner = lane // (SHARE * BLOCK_ROWS)
        last = jnp.full((1, TILE_ROWS), blocks[0], jnp.int32)
        for n in range(1, TILE_BLOCKS):
            last = jnp.where(owner == n, blocks[n], last)
        last = last * BLOCK_ROWS + (lane & (BLOCK_ROWS - 1))
        start = jnp.zeros((1, TILE_ROWS), jnp.int32)
        tile_start = jnp.int32(0)
        for n in range(DOCS):
            end = doc_ends[n]
            start = jnp.where(end <= last, end, start)
            tile_start = jnp.where(end <= blocks[0] * BLOCK_ROWS, end, tile_start)
        first_tile = tile_start // KEY_TILE
        last_tile = (blocks[-1] * BLOCK_ROWS + BLOCK_ROWS - 1) // KEY_TILE

        def totals(key_tile, state):
            top, total, weighted = state
            rows = pl.ds(pl.multiple_of(key_tile * KEY_TILE, KEY_TILE), KEY_TILE)
            scores = jnp.dot(k_pack[rows, :], q_turned, preferred_element_type=F32)
            prob_grad = jnp.dot(v_pack[rows, :], g_turned, preferred_element_type=F32)
            position = key_iota + key_tile * KEY_TILE
            allowed = (position >= start) & (position <= last)
            scores = jnp.where(allowed, scores, -1e30)
            new_top = jnp.maximum(top, jnp.max(scores, axis=0, keepdims=True))
            weights = jnp.exp2((scores - new_top) * EXP2_SCALE)
            fade = jnp.exp2((top - new_top) * EXP2_SCALE)
            total = total * fade + jnp.sum(weights, axis=0, keepdims=True)
            weighted = weighted * fade + jnp.sum(weights * prob_grad, axis=0, keepdims=True)
            slot = key_tile - first_tile
            exps[slot] = weights
            probs[slot] = prob_grad
            maxes[slot] = jnp.broadcast_to(new_top, (8, TILE_ROWS))
            return new_top, total, weighted

        top, total, weighted = lax.fori_loop(
            first_tile,
            last_tile + 1,
            totals,
            (jnp.full((1, TILE_ROWS), -1e20, F32), jnp.zeros((1, TILE_ROWS), F32), jnp.zeros((1, TILE_ROWS), F32)),
        )
        scale_row = 1.0 / total
        delta = weighted * scale_row

        def gradients(key_tile, dq_turned):
            rows = pl.ds(pl.multiple_of(key_tile * KEY_TILE, KEY_TILE), KEY_TILE)
            slot = key_tile - first_tile
            factor = jnp.exp2((maxes[slot][:1] - top) * EXP2_SCALE) * scale_row
            weights = exps[slot] * factor
            score_grad = (weights * (probs[slot] - delta)).astype(BF16)
            dv_acc[rows, :] += jnp.dot(weights.astype(BF16), g_low, preferred_element_type=F32)
            dk_acc[rows, :] += jnp.dot(score_grad, q_low, preferred_element_type=F32)
            return dq_turned + jnp.dot(k_turned[key_tile], score_grad, preferred_element_type=F32)

        dq_turned = lax.fori_loop(
            first_tile, last_tile + 1, gradients, jnp.zeros((HEAD_DIM, TILE_ROWS), F32)
        )
        dq = jnp.transpose(dq_turned) * SCORE_SCALE
        for n, slot in enumerate(slots):
            for h in range(SHARE):
                part = (n * SHARE + h) * BLOCK_ROWS
                dq_acc[
                    pl.ds(pl.multiple_of(slot * BLOCK_ROWS, BLOCK_ROWS), BLOCK_ROWS),
                    h * HEAD_DIM : (h + 1) * HEAD_DIM,
                ] = dq[part : part + BLOCK_ROWS]
        return carry

    lax.fori_loop(0, TILES, query_tile, 0)

    def finish_queries(step, carry):
        dq_ref[step] = dq_acc[pl.ds(pl.multiple_of(step * RUN, RUN), RUN), :].astype(BF16)
        return carry

    lax.fori_loop(0, PEERS, finish_queries, 0, unroll=2)

    def finish_keys(step, carry):
        first = pl.multiple_of(packed_to[2 * step] * BLOCK_ROWS, BLOCK_ROWS)
        second = pl.multiple_of(packed_to[2 * step + 1] * BLOCK_ROWS, BLOCK_ROWS)
        for src, dst, scale in ((dk_acc, dk_ref, SCORE_SCALE), (dv_acc, dv_ref, 1.0)):
            rows = jnp.concatenate([src[pl.ds(first, BLOCK_ROWS), :], src[pl.ds(second, BLOCK_ROWS), :]], axis=0)
            dst[step] = (rows * scale).astype(BF16)
        return carry

    lax.fori_loop(0, GROUP_BLOCKS // 2, finish_keys, 0, unroll=8)


def attention(tables, queries, grads, keys, values):
    narrow = jax.ShapeDtypeStruct((GROUP_BLOCKS // 2, RUN, HEAD_DIM), BF16)
    return pl.pallas_call(
        attention_kernel,
        name="attention",
        out_shape=(jax.ShapeDtypeStruct((PEERS, RUN, UNIT), BF16), narrow, narrow),
        in_specs=[pl.BlockSpec(memory_space=pltpu.SMEM)] * 5 + [pl.BlockSpec(memory_space=pltpu.VMEM)] * 4,
        out_specs=[pl.BlockSpec(memory_space=pltpu.VMEM)] * 3,
        scratch_shapes=[
            pltpu.VMEM((GROUP_TOKENS, HEAD_DIM), BF16),
            pltpu.VMEM((GROUP_TOKENS, HEAD_DIM), BF16),
            pltpu.VMEM((KEY_TILES, HEAD_DIM, KEY_TILE), BF16),
            pltpu.VMEM((GROUP_TOKENS, HEAD_DIM), F32),
            pltpu.VMEM((GROUP_TOKENS, HEAD_DIM), F32),
            pltpu.VMEM((PLANE_BLOCKS * BLOCK_ROWS, UNIT), F32),
            pltpu.VMEM((KEY_TILES, KEY_TILE, TILE_ROWS), F32),
            pltpu.VMEM((KEY_TILES, KEY_TILE, TILE_ROWS), F32),
            pltpu.VMEM((KEY_TILES, 8, TILE_ROWS), F32),
        ],
        compiler_params=pltpu.CompilerParams(vmem_limit_bytes=48 * 1024 * 1024),
    )(*tables, queries, grads, keys, values)


def collect_kernel(
    dq_ref,
    dk_ref,
    dv_ref,
    dq_out,
    dk_out,
    dv_out,
    inbox,
    total,
    in_send,
    in_recv,
    own_sem,
    ring_send,
    ring_recv,
):
    group, head, plane = place()
    me = group * KV_HEADS + head
    greet(group, head, plane)
    here = device_of(group, head, plane)

    def home_of(ref, width):
        return ref.at[
            pl.ds(pl.multiple_of(group * RUN, RUN), RUN), pl.ds(pl.multiple_of(head * width, width), width)
        ]

    def send_wide(step, carry):
        peer = lax.rem(me + step, PEERS)
        remote(
            dq_ref.at[peer],
            home_of(dq_out, UNIT),
            in_send.at[2],
            in_recv.at[2],
            device_of(peer // KV_HEADS, lax.rem(peer, KV_HEADS), plane),
        ).start()
        return carry

    parts = (dk_ref, dv_ref)

    def ring(way, step, n, src):
        target = lax.rem(plane + (1 if way == 0 else PLANES - 1), PLANES)
        return remote(
            src,
            inbox.at[way, n, step],
            ring_send.at[way, step, n],
            ring_recv.at[way, step, n],
            device_of(group, head, target),
        )

    def chunk_at(way, step):
        distance = 4 - step
        return lax.rem(plane + (distance if way == 0 else PLANES - distance), PLANES)

    started = []
    for step in range(4):
        for way in range(2):
            chunk = chunk_at(way, step)
            for n in range(2):
                if step == 0 and n != way:
                    continue
                if step == 0 or (step == 1 and n != way):
                    copy = ring(way, step, n, parts[n].at[chunk])
                else:
                    held = inbox.at[way, n, step - 1]
                    ring(way, step - 1, n, held).wait_recv()
                    held[...] = (held[...].astype(F32) + parts[n][chunk].astype(F32)).astype(BF16)
                    copy = ring(way, step, n, held)
                copy.start()
                started.append(copy)
        if step == 0:
            own_wide = pltpu.make_async_copy(dq_ref.at[me], home_of(dq_out, UNIT), own_sem.at[2])
            own_wide.start()
            lax.fori_loop(1, PEERS, send_wide, 0)
    for n in range(2):
        for way in range(2):
            ring(way, 3, n, inbox.at[way, n, 3]).wait_recv()
        total[n] = (
            parts[n][plane].astype(F32) + inbox[0, n, 3].astype(F32) + inbox[1, n, 3].astype(F32)
        ).astype(BF16)

    outs = (dk_out, dv_out)

    def send_narrow(step, carry):
        peer = lax.rem(me + step, PEERS)
        for n in range(2):
            remote(
                total.at[n, peer],
                home_of(outs[n], HEAD_DIM),
                in_send.at[n],
                in_recv.at[n],
                device_of(peer // KV_HEADS, lax.rem(peer, KV_HEADS), plane),
            ).start()
        return carry

    lax.fori_loop(1, PEERS, send_narrow, 0)
    own = [pltpu.make_async_copy(total.at[n, me], home_of(outs[n], HEAD_DIM), own_sem.at[n]) for n in range(2)]
    for copy in own:
        copy.start()
    for copy in started:
        copy.wait_send()
    own_wide.wait()
    rest_wide = remote(
        dq_ref.at[pl.ds(0, PEERS - 1)], dq_ref.at[pl.ds(0, PEERS - 1)], in_send.at[2], in_recv.at[2], here
    )
    rest_wide.wait_send()
    rest_wide.wait_recv()
    for n in range(2):
        rest = remote(
            total.at[n, pl.ds(0, PEERS - 1)], total.at[n, pl.ds(0, PEERS - 1)], in_send.at[n], in_recv.at[n], here
        )
        rest.wait_send()
        rest.wait_recv()
        own[n].wait()


def collect(dq, dk, dv):
    return pl.pallas_call(
        collect_kernel,
        name="collect",
        out_shape=(
            jax.ShapeDtypeStruct((GROUPS * RUN, KV_HEADS * UNIT), BF16),
            jax.ShapeDtypeStruct((GROUPS * RUN, KV_HEADS * HEAD_DIM), BF16),
            jax.ShapeDtypeStruct((GROUPS * RUN, KV_HEADS * HEAD_DIM), BF16),
        ),
        in_specs=[
            pl.BlockSpec(memory_space=pl.ANY),
            pl.BlockSpec(memory_space=pltpu.VMEM),
            pl.BlockSpec(memory_space=pltpu.VMEM),
        ],
        out_specs=[pl.BlockSpec(memory_space=pl.ANY)] * 3,
        scratch_shapes=[
            pltpu.VMEM((2, 2, 4, PEERS, RUN, HEAD_DIM), BF16),
            pltpu.VMEM((2, PEERS, RUN, HEAD_DIM), BF16),
            pltpu.SemaphoreType.DMA((3,)),
            pltpu.SemaphoreType.DMA((3,)),
            pltpu.SemaphoreType.DMA((3,)),
            pltpu.SemaphoreType.DMA((2, 4, 2)),
            pltpu.SemaphoreType.DMA((2, 4, 2)),
        ],
        compiler_params=pltpu.CompilerParams(
            collective_id=1, has_side_effects=True, vmem_limit_bytes=32 * 1024 * 1024
        ),
    )(dq, dk, dv)


def tables_of(block_target, doc_lengths):
    group, _, plane = place()
    targets = lax.dynamic_slice(block_target, (0, 0, 2 * group), (GROUPS, PEERS, 2)) - group * GROUP_BLOCKS
    targets = targets.reshape(GROUPS, 2, PLANES, 2, 2).transpose(2, 0, 1, 3, 4)
    packed_to = targets.reshape(GROUP_BLOCKS)
    count = jnp.arange(GROUP_BLOCKS, dtype=jnp.int32)
    packed_from = jnp.sum(jnp.where(packed_to[None, :] == count[:, None], count[None, :], 0), axis=1)
    mine = lax.dynamic_index_in_dim(targets.reshape(PLANES, PLANE_BLOCKS), plane, 0, keepdims=False)
    rank = jnp.sum((mine[None, :] < mine[:, None]).astype(jnp.int32), axis=1)
    small = jnp.arange(PLANE_BLOCKS, dtype=jnp.int32)
    hit = rank[None, :] == small[:, None]
    query_order = jnp.sum(jnp.where(hit, small[None, :], 0), axis=1)
    query_block = jnp.sum(jnp.where(hit, mine[None, :], 0), axis=1)
    doc_ends = jnp.cumsum(doc_lengths[0])
    return packed_from, packed_to, query_order, query_block, doc_ends


def on_device(query_rows, key_rows, value_rows, output_grad, block_target, doc_lengths):
    tables = tables_of(block_target, doc_lengths)
    queries, grads, keys, values = scatter(query_rows, output_grad, key_rows, value_rows)
    pairs = (GROUP_BLOCKS // 2, RUN, HEAD_DIM)
    dq, dk, dv = attention(tables, queries, grads, keys.reshape(pairs), values.reshape(pairs))
    planes = (PLANES, PEERS, RUN, HEAD_DIM)
    return collect(dq, dk.reshape(planes), dv.reshape(planes))


def solution(mesh):
    in_specs = (
        P(("grp", "ctx"), None),
        P(("grp", "ctx"), None),
        P(("grp", "ctx"), None),
        P(("grp", "ctx"), None),
        P(),
        P("grp", None),
    )
    out_specs = (P(("grp", "ctx"), None), P(("grp", "ctx"), None), P(("grp", "ctx"), None))
    return jax.shard_map(
        on_device, mesh=mesh, in_specs=in_specs, out_specs=out_specs, check_vma=False
    )
```

time: 506 us -> 122 us (0.24)
  the two profiles are of different devices: /device:TPU:32 before, /device:TPU:1 now
where the time goes in v1:
time: 122 us
  Pallas kernels  114 us (93%)
  local copies, waits for them, and re-layouts  7.09 us (6%)
    pallas_call x1, Pallas kernels, collect(): pl.pallas_call(collect_kernel, name='collect', out_shape=(jax.ShapeDtypeS...  45.3 us
    pallas_call x1, Pallas kernels, scatter(): pl.pallas_call(scatter_kernel, name='scatter', out_shape=(wide, wide, nar...  42.9 us
    pallas_call x1, Pallas kernels, attention(): pl.pallas_call(attention_kernel, name='attention', out_shape=(jax.ShapeDt...  25.5 us
    unnamed x12, local copies, waits for them, and re-layouts  6.25 us

profile of v1, /device:TPU:1, one launch (start us, length us, event | category | flops | bytes accessed | tf_op | source)
XLA Modules:
  0.0 122.1 jit_solution(1545398028064914426)
XLA Ops:
  0.6 0.0 copy-start
  0.7 0.8 copy-done
  1.5 0.0 copy-start.3
  1.5 0.6 copy-done.3
  2.1 0.1 copy.22
  2.3 0.1 reduce.1.doc_ends
  2.4 0.1 copy.23
  2.5 0.1 copy.21
  2.6 0.2 dynamic-slice_reduce_fusion
  2.8 0.2 convert_reduce_fusion
  2.9 0.1 select_reduce_fusion.1
  3.1 0.3 copy.20
  3.3 0.2 eq.30.packed_to
  3.5 0.2 select_reduce_fusion.packed_from
  3.7 42.9 %scatter.1 = (bf16[32,16,1024]{2,1,0:T(8,128)(2,1)}, bf16[32,16,1024]{2,1,0:T(8,128)(2,1)}, bf16[8,32,16,128]{3,2,1,0:T(8,128)(2,1)}, bf16[8,32,16,128]{3,2,1,0:T(8,128)(2,1)}) custom-call(bf16[128,4096]{1,0:T(8,128)(2,1)} %q_ref.1, bf16[128,4096]{1,0:T(8,128)(2,1)} %g_ref.1, bf16[128,512]{1,0:T(8,128)(2,1)} %k_ref.1, bf16[128,512]{1,0:T(8,128)(2,1)} %v_ref.1), custom_call_target="tpu_custom_call" | custom-call | tf_op jit(solution)/shard_map/scatter/pallas_call | solution.py:182
  46.7 0.0 copy-start.1
  46.7 1.2 copy-done.1
  47.9 0.0 copy-start.2
  47.9 1.2 %copy-done.2 = bf16[32,16,1024]{2,1,0:T(8,128)(2,1)S(1)} copy-done((bf16[32,16,1024]{2,1,0:T(8,128)(2,1)S(1)}, bf16[32,16,1024]{2,1,0:T(8,128)(2,1)}, u32[]{:S(2)}) %copy-start.2) | copy-done | bytes 1048600
  49.1 25.5 %attention.1 = (bf16[32,16,1024]{2,1,0:T(8,128)(2,1)S(1)}, bf16[256,16,128]{2,1,0:T(8,128)(2,1)S(1)}, bf16[256,16,128]{2,1,0:T(8,128)(2,1)S(1)}) custom-call(s32[512]{0:T(512)S(1)} %select_reduce_fusion.packed_from, s32[512]{0:T(512)S(1)} %eq.30.packed_to, s32[64]{0:T(128)S(1)} %get-tuple-element.18.query_order, s32[64]{0:T(128)S(1)} %get-tuple-element.17.query_block, ...), custom_call_target="tpu_custom_call" | custom-call | tf_op jit(solution)/shard_map/attention/pallas_call | solution.py:353
  74.6 45.3 %collect.1 = (bf16[128,4096]{1,0:T(8,128)(2,1)S(1)}, bf16[128,512]{1,0:T(8,128)(2,1)S(1)}, bf16[128,512]{1,0:T(8,128)(2,1)S(1)}) custom-call(bf16[32,16,1024]{2,1,0:T(8,128)(2,1)S(1)} %get-tuple-element.14.dq_ref, bf16[8,32,16,128]{3,2,1,0:T(8,128)(2,1)S(1)} %bitcast.9, bf16[8,32,16,128]{3,2,1,0:T(8,128)(2,1)S(1)} %bitcast.10), custom_call_target="tpu_custom_call" | custom-call | tf_op jit(solution)/shard_map/collect/pallas_call | solution.py:489
  119.9 1.0 copy.27
  120.8 0.7 copy.28
  121.5 0.7 copy.29
  (3 shorter events, 0.0 us)
Async XLA Ops:
  0.6 0.8 copy-start
  1.5 0.7 copy-start.3
  46.7 1.2 %copy-start.1 = (bf16[32,16,1024]{2,1,0:T(8,128)(2,1)S(1)}, bf16[32,16,1024]{2,1,0:T(8,128)(2,1)}, u32[]{:S(2)}) copy-start(bf16[32,16,1024]{2,1,0:T(8,128)(2,1)} %get-tuple-element.10.q_ref) | copy-start | bytes 3145732
  47.9 1.2 %copy-start.2 = (bf16[32,16,1024]{2,1,0:T(8,128)(2,1)S(1)}, bf16[32,16,1024]{2,1,0:T(8,128)(2,1)}, u32[]{:S(2)}) copy-start(bf16[32,16,1024]{2,1,0:T(8,128)(2,1)} %get-tuple-element.11.g_ref) | copy-start | bytes 3145732

commit v2 on v1

v2 whole, which is shorter than its diff:
```python
import jax
import jax.numpy as jnp
from jax import lax
from jax.experimental import pallas as pl
from jax.experimental.pallas import tpu as pltpu
from jax.sharding import PartitionSpec as P

KV_HEADS = 4
HEAD_DIM = 128
SHARE = 8
BLOCK_ROWS = 8
GROUPS = 8
PLANES = 8
PEERS = 32
RUN = 16
UNIT = SHARE * HEAD_DIM
GROUP_BLOCKS = 512
GROUP_TOKENS = 4096
PLANE_BLOCKS = 64
DOCS = 16
TILE_BLOCKS = 4
TILE_ROWS = TILE_BLOCKS * SHARE * BLOCK_ROWS
TILES = PLANE_BLOCKS // TILE_BLOCKS
CHUNK = 128
CHUNKS = GROUP_TOKENS // CHUNK
FIXED_MAX = 7
TOGETHER = 2
UNROLL_PREP = 2
SCORE_SCALE = HEAD_DIM**-0.5
EXP2_SCALE = SCORE_SCALE * 1.4426950408889634
PARTS = 4
PART = PEERS // PARTS
WIDE_STEPS = (1, 32, 32, 32, 32)
MESH = pl.DeviceIdType.MESH
F32 = jnp.float32
BF16 = jnp.bfloat16


def place():
    group = lax.axis_index("grp")
    ctx = lax.axis_index("ctx")
    y_hi = ctx // 16
    plane = (ctx // 2) % PLANES
    core = ctx % 2
    head = y_hi * 2 + core
    return group, head, plane


def device_of(group, head, plane):
    return {"grp": group, "ctx": (head // 2) * 16 + plane * 2 + head % 2}


def greet(group, head, plane):
    barrier = pltpu.get_barrier_semaphore()
    me = group * KV_HEADS + head

    def one(step, carry):
        peer = lax.rem(me + step, PEERS)
        pl.semaphore_signal(
            barrier,
            inc=1,
            device_id=device_of(peer // KV_HEADS, lax.rem(peer, KV_HEADS), plane),
            device_id_type=MESH,
        )
        return carry

    lax.fori_loop(1, PEERS, one, 0)
    for by in (1, PLANES - 1):
        pl.semaphore_signal(
            barrier,
            inc=1,
            device_id=device_of(group, head, lax.rem(plane + by, PLANES)),
            device_id_type=MESH,
        )
    pl.semaphore_wait(barrier, PEERS - 1 + 2)


def remote(src, dst, send, recv, device):
    return pltpu.make_async_remote_copy(
        src_ref=src, dst_ref=dst, send_sem=send, recv_sem=recv, device_id=device, device_id_type=MESH
    )


def scatter_kernel(
    q_ref, g_ref, k_ref, v_ref, q_out, g_out, k_out, v_out, send_sem, narrow_recv, wide_recv, own_sem, ring_send, ring_recv
):
    group, head, plane = place()
    me = group * KV_HEADS + head
    greet(group, head, plane)
    here = device_of(group, head, plane)
    narrow = ((k_ref, k_out), (v_ref, v_out))
    wide = ((q_ref, q_out), (g_ref, g_out))

    def run_of(ref, to_group, to_head, width):
        return ref.at[
            pl.ds(pl.multiple_of(to_group * RUN, RUN), RUN),
            pl.ds(pl.multiple_of(to_head * width, width), width),
        ]

    def send_narrow(step, carry):
        peer = lax.rem(me + step, PEERS)
        to_group, to_head = peer // KV_HEADS, lax.rem(peer, KV_HEADS)
        for n, (src, dst) in enumerate(narrow):
            remote(
                run_of(src, to_group, to_head, HEAD_DIM),
                dst.at[plane, step],
                send_sem.at[n],
                narrow_recv.at[n, step // PART],
                device_of(to_group, to_head, plane),
            ).start()
        return carry

    def send_wide(step, carry):
        peer = lax.rem(me + step, PEERS)
        to_group, to_head = peer // KV_HEADS, lax.rem(peer, KV_HEADS)
        for n, (src, dst) in enumerate(wide):
            remote(
                run_of(src, to_group, to_head, UNIT),
                dst.at[step],
                send_sem.at[2 + n],
                wide_recv.at[n],
                device_of(to_group, to_head, plane),
            ).start()
        return carry

    own = [
        pltpu.make_async_copy(run_of(src, group, head, HEAD_DIM), dst.at[plane, 0], own_sem.at[n])
        for n, (src, dst) in enumerate(narrow)
    ] + [
        pltpu.make_async_copy(run_of(src, group, head, UNIT), dst.at[0], own_sem.at[2 + n])
        for n, (src, dst) in enumerate(wide)
    ]
    own[0].start()
    own[1].start()
    lax.fori_loop(1, PEERS, send_narrow, 0)
    own[2].start()
    own[3].start()

    def ring(way, step, n, part):
        chunk = lax.rem(plane + (PLANES - step if way == 0 else step), PLANES)
        target = lax.rem(plane + (1 if way == 0 else PLANES - 1), PLANES)
        piece = narrow[n][1].at[chunk, pl.ds(part * PART, PART)]
        return remote(
            piece,
            piece,
            ring_send.at[way, n],
            ring_recv.at[way, step, n, part],
            device_of(group, head, target),
        )

    for step in range(4):
        lax.fori_loop(WIDE_STEPS[step], WIDE_STEPS[step + 1], send_wide, 0)
        for part in range(PARTS):
            for n in range(2):
                if step == 0:
                    if part == 0:
                        own[n].wait()
                    landed = narrow[n][1].at[plane, pl.ds(part * PART, PART - (part == 0))]
                    remote(landed, landed, send_sem.at[n], narrow_recv.at[n, part], here).wait_recv()
                for way in range(2):
                    if step == 3 and n != way:
                        continue
                    if step > 0:
                        ring(way, step - 1, n, part).wait_recv()
                    ring(way, step, n, part).start()
    for part in range(PARTS):
        for way in range(2):
            ring(way, 2, 1 - way, part).wait_recv()
    for part in range(PARTS):
        for way in range(2):
            ring(way, 3, way, part).wait_recv()
    for way in range(2):
        for n in range(2):
            sent = narrow[n][1].at[pl.ds(0, 4 if n == way else 3)]
            remote(sent, sent, ring_send.at[way, n], ring_recv.at[way, 0, n, 0], here).wait_send()
    for n in range(2):
        sent = narrow[n][1].at[0, pl.ds(0, PEERS - 1)]
        remote(sent, sent, send_sem.at[n], narrow_recv.at[n, 0], here).wait_send()
        own[2 + n].wait()
        landed = wide[n][1].at[pl.ds(0, PEERS - 1)]
        rest = remote(landed, landed, send_sem.at[2 + n], wide_recv.at[n], here)
        rest.wait_recv()
        rest.wait_send()


def scatter(query_rows, output_grad, key_rows, value_rows):
    wide = jax.ShapeDtypeStruct((PEERS, RUN, UNIT), BF16)
    narrow = jax.ShapeDtypeStruct((PLANES, PEERS, RUN, HEAD_DIM), BF16)
    return pl.pallas_call(
        scatter_kernel,
        name="scatter",
        out_shape=(wide, wide, narrow, narrow),
        in_specs=[pl.BlockSpec(memory_space=pl.ANY)] * 4,
        out_specs=[pl.BlockSpec(memory_space=pl.ANY)] * 4,
        scratch_shapes=[
            pltpu.SemaphoreType.DMA((4,)),
            pltpu.SemaphoreType.DMA((2, PARTS)),
            pltpu.SemaphoreType.DMA((2,)),
            pltpu.SemaphoreType.DMA((4,)),
            pltpu.SemaphoreType.DMA((2, 2)),
            pltpu.SemaphoreType.DMA((2, 4, 2, PARTS)),
        ],
        compiler_params=pltpu.CompilerParams(
            collective_id=0, has_side_effects=True, vmem_limit_bytes=2 * 1024 * 1024
        ),
    )(query_rows, output_grad, key_rows, value_rows)


def attention_kernel(
    target_ref,
    length_ref,
    q_ref,
    g_ref,
    k_ref,
    v_ref,
    dq_ref,
    dk_ref,
    dv_ref,
    packed_to,
    holder,
    query_order,
    query_block,
    doc_ends,
    k_pack,
    v_pack,
    q_tiles,
    g_tiles,
    bounds,
    spans,
    k_turned,
    dk_acc,
    dv_acc,
    dq_turned,
    dq_acc,
    exps,
    probs,
    maxes,
):
    def half_of(pair, which):
        wide = pair.astype(F32)
        return jnp.where(which == 0, wide[:BLOCK_ROWS], wide[BLOCK_ROWS:])

    group, head, plane = place()
    me = group * KV_HEADS + head

    def target_of(source, from_plane, which):
        ctx = ((source >> 1) & 1) * 16 + (source & 1) + from_plane * 2
        return target_ref[source >> 2, ctx, 2 * group + which] - group * GROUP_BLOCKS

    def clear(step, carry):
        holder[step] = 0
        return carry

    lax.fori_loop(0, GROUP_BLOCKS, clear, 0, unroll=16)

    def hold(slot, carry):
        for which in range(2):
            holder[target_of((me - slot) & (PEERS - 1), plane, which)] = 2 * slot + which + 1
        return carry

    lax.fori_loop(0, PEERS, hold, 0, unroll=4)

    end = jnp.int32(0)
    for n in range(DOCS):
        end = end + length_ref[0, n]
        doc_ends[n] = end

    def pack(source, carry):
        slot = (me - source) & (PEERS - 1)
        for from_plane in range(PLANES):
            pair = from_plane * PEERS + slot
            keys = k_ref[pair].astype(F32)
            values = v_ref[pair].astype(F32)
            for which in range(2):
                block = target_of(source, from_plane, which)
                packed_to[2 * pair + which] = block
                rows = pl.ds(pl.multiple_of(block * BLOCK_ROWS, BLOCK_ROWS), BLOCK_ROWS)
                half = slice(which * BLOCK_ROWS, (which + 1) * BLOCK_ROWS)
                dk_acc[rows, :] = keys[half]
                dv_acc[rows, :] = values[half]
        return carry

    lax.fori_loop(0, PEERS, pack, 0, unroll=2)

    def turn(step, found):
        rows = pl.ds(pl.multiple_of(step * CHUNK, CHUNK), CHUNK)
        keys = dk_acc[rows, :]
        k_pack[rows, :] = keys.astype(BF16)
        k_turned[step] = jnp.transpose(keys).astype(BF16)
        v_pack[rows, :] = dv_acc[rows, :].astype(BF16)
        dk_acc[rows, :] = jnp.zeros((CHUNK, HEAD_DIM), F32)
        dv_acc[rows, :] = jnp.zeros((CHUNK, HEAD_DIM), F32)
        for n in range(CHUNK // BLOCK_ROWS):
            block = step * (CHUNK // BLOCK_ROWS) + n
            slot = holder[block]
            query_order[found] = slot - 1
            query_block[found] = block
            found = found + jnp.where(slot > 0, 1, 0)
        return found

    lax.fori_loop(0, CHUNKS, turn, jnp.int32(0), unroll=2)

    lane = lax.broadcasted_iota(jnp.int32, (1, TILE_ROWS), 1)
    owner = lane // (SHARE * BLOCK_ROWS)

    def prepare(tile, carry):
        slots = [query_order[tile * TILE_BLOCKS + n] for n in range(TILE_BLOCKS)]
        blocks = [query_block[tile * TILE_BLOCKS + n] for n in range(TILE_BLOCKS)]
        for src, dst in ((q_ref, q_tiles), (g_ref, g_tiles)):
            parts = []
            for slot in slots:
                rows = half_of(src[slot >> 1], slot & 1)
                parts += [rows[:, h * HEAD_DIM : (h + 1) * HEAD_DIM] for h in range(SHARE)]
            dst[tile] = jnp.concatenate(parts, axis=0).astype(BF16)
        last = jnp.full((1, TILE_ROWS), blocks[0], jnp.int32)
        for n in range(1, TILE_BLOCKS):
            last = jnp.where(owner == n, blocks[n], last)
        last = last * BLOCK_ROWS + (lane & (BLOCK_ROWS - 1))
        start = jnp.zeros((1, TILE_ROWS), jnp.int32)
        tile_start = jnp.int32(0)
        for n in range(DOCS):
            end = doc_ends[n]
            start = jnp.where(end <= last, end, start)
            tile_start = jnp.where(end <= blocks[0] * BLOCK_ROWS, end, tile_start)
        bounds[tile, 0:1] = start
        bounds[tile, 1:2] = last
        first_chunk = tile_start // CHUNK
        spans[2 * tile] = first_chunk
        spans[2 * tile + 1] = (blocks[-1] * BLOCK_ROWS + BLOCK_ROWS - 1) // CHUNK - first_chunk + 1
        return carry

    lax.fori_loop(0, TILES, prepare, 0, unroll=UNROLL_PREP)

    key_iota = lax.broadcasted_iota(jnp.int32, (CHUNK, TILE_ROWS), 0)
    no_sum = jnp.zeros((8, TILE_ROWS), F32)

    def fold(array, op):
        return op(array.reshape(CHUNK // 8, 8, TILE_ROWS), axis=0)

    def rows_of(chunk):
        return pl.ds(pl.multiple_of(chunk * CHUNK, CHUNK), CHUNK)

    def against(rows_ref, chunk, tile_rows):
        return lax.dot_general(
            rows_ref[rows_of(chunk), :], tile_rows, (((1,), (1,)), ((), ())), preferred_element_type=F32
        )

    def masked(scores, chunk, start, last):
        position = key_iota + chunk * CHUNK
        return jnp.where((position >= start) & (position <= last), scores, -1e30)

    def put_keys(chunk, weights, score_grad, q_low, g_low):
        rows = rows_of(chunk)
        dv_acc[rows, :] += jnp.dot(weights.astype(BF16), g_low, preferred_element_type=F32)
        dk_acc[rows, :] += jnp.dot(score_grad, q_low, preferred_element_type=F32)
        return jnp.dot(k_turned[chunk], score_grad, preferred_element_type=F32)

    def query_tiles(step, carry):
        tiles = [step * TOGETHER + n for n in range(TOGETHER)]
        firsts = [spans[2 * tile] for tile in tiles]
        counts = [spans[2 * tile + 1] for tile in tiles]
        most = counts[0]
        for count in counts[1:]:
            most = jnp.maximum(most, count)

        def fixed(chunks):
            begins = [jnp.minimum(first, CHUNKS - chunks) for first in firsts]
            ways = range(TOGETHER)
            q_low = [q_tiles[tile] for tile in tiles]
            g_low = [g_tiles[tile] for tile in tiles]
            start = [bounds[tile, 0:1] for tile in tiles]
            last = [bounds[tile, 1:2] for tile in tiles]
            top = [jnp.full((8, TILE_ROWS), -1e30, F32)] * TOGETHER
            for n in range(chunks):
                for w in ways:
                    chunk = begins[w] + n
                    scores = masked(against(k_pack, chunk, q_low[w]), chunk, start[w], last[w])
                    exps[w * FIXED_MAX + n] = scores
                    top[w] = jnp.maximum(top[w], fold(scores, jnp.max))
            top = [jnp.max(t, axis=0, keepdims=True) for t in top]
            total, weighted = [no_sum] * TOGETHER, [no_sum] * TOGETHER
            for n in range(chunks):
                for w in ways:
                    prob_grad = against(v_pack, begins[w] + n, g_low[w])
                    weights = jnp.exp2((exps[w * FIXED_MAX + n] - top[w]) * EXP2_SCALE)
                    total[w] += fold(weights, jnp.sum)
                    weighted[w] += fold(weights * prob_grad, jnp.sum)
                    exps[w * FIXED_MAX + n] = weights
                    probs[w * FIXED_MAX + n] = prob_grad
            factor = [1.0 / jnp.sum(t, axis=0, keepdims=True) for t in total]
            delta = [jnp.sum(t, axis=0, keepdims=True) * f for t, f in zip(weighted, factor)]
            dq = [jnp.zeros((HEAD_DIM, TILE_ROWS), F32)] * TOGETHER
            for n in range(chunks):
                for w in ways:
                    weights = exps[w * FIXED_MAX + n] * factor[w]
                    score_grad = (weights * (probs[w * FIXED_MAX + n] - delta[w])).astype(BF16)
                    dq[w] += put_keys(begins[w] + n, weights, score_grad, q_low[w], g_low[w])
            for w in ways:
                dq_turned[tiles[w]] = dq[w]

        for chunks in range(1, FIXED_MAX + 1):

            @pl.when(most == chunks)
            def _():
                fixed(chunks)

        @pl.when(most > FIXED_MAX)
        def _():
            for tile, first, count in zip(tiles, firsts, counts):
                any_length(tile, first, count)

        return carry

    def any_length(tile, first, count):
        q_low, g_low = q_tiles[tile], g_tiles[tile]
        start, last = bounds[tile, 0:1], bounds[tile, 1:2]

        def totals(slot, state):
            top, total, weighted = state
            chunk = first + slot
            scores = masked(against(k_pack, chunk, q_low), chunk, start, last)
            prob_grad = against(v_pack, chunk, g_low)
            new_top = jnp.maximum(top, jnp.max(scores, axis=0, keepdims=True))
            weights = jnp.exp2((scores - new_top) * EXP2_SCALE)
            fade = jnp.exp2((top - new_top) * EXP2_SCALE)
            total = total * fade + jnp.sum(weights, axis=0, keepdims=True)
            weighted = weighted * fade + jnp.sum(weights * prob_grad, axis=0, keepdims=True)
            exps[slot] = weights
            probs[slot] = prob_grad
            maxes[slot] = jnp.broadcast_to(new_top, (8, TILE_ROWS))
            return new_top, total, weighted

        top, total, weighted = lax.fori_loop(
            0, count, totals, (jnp.full((1, TILE_ROWS), -1e20, F32), no_sum[:1], no_sum[:1])
        )
        scale_row = 1.0 / total
        delta = weighted * scale_row

        def gradients(slot, dq):
            factor = jnp.exp2((maxes[slot][:1] - top) * EXP2_SCALE) * scale_row
            weights = exps[slot] * factor
            score_grad = (weights * (probs[slot] - delta)).astype(BF16)
            return dq + put_keys(first + slot, weights, score_grad, q_low, g_low)

        dq_turned[tile] = lax.fori_loop(0, count, gradients, jnp.zeros((HEAD_DIM, TILE_ROWS), F32))

    lax.fori_loop(0, TILES // TOGETHER, query_tiles, 0)

    def place_queries(tile, carry):
        dq = jnp.transpose(dq_turned[tile]) * SCORE_SCALE
        for n in range(TILE_BLOCKS):
            rows = pl.ds(pl.multiple_of(query_order[tile * TILE_BLOCKS + n] * BLOCK_ROWS, BLOCK_ROWS), BLOCK_ROWS)
            for h in range(SHARE):
                part = (n * SHARE + h) * BLOCK_ROWS
                dq_acc[rows, h * HEAD_DIM : (h + 1) * HEAD_DIM] = dq[part : part + BLOCK_ROWS]
        return carry

    lax.fori_loop(0, TILES, place_queries, 0, unroll=UNROLL_PREP)

    def finish_queries(step, carry):
        dq_ref[step] = dq_acc[pl.ds(pl.multiple_of(step * RUN, RUN), RUN), :].astype(BF16)
        return carry

    lax.fori_loop(0, PEERS, finish_queries, 0, unroll=2)

    def finish_keys(step, carry):
        first = pl.multiple_of(packed_to[2 * step] * BLOCK_ROWS, BLOCK_ROWS)
        second = pl.multiple_of(packed_to[2 * step + 1] * BLOCK_ROWS, BLOCK_ROWS)
        for src, dst, scale in ((dk_acc, dk_ref, SCORE_SCALE), (dv_acc, dv_ref, 1.0)):
            rows = jnp.concatenate([src[pl.ds(first, BLOCK_ROWS), :], src[pl.ds(second, BLOCK_ROWS), :]], axis=0)
            dst[step] = (rows * scale).astype(BF16)
        return carry

    lax.fori_loop(0, GROUP_BLOCKS // 2, finish_keys, 0, unroll=8)


def attention(block_target, doc_lengths, queries, grads, keys, values):
    narrow = jax.ShapeDtypeStruct((GROUP_BLOCKS // 2, RUN, HEAD_DIM), BF16)
    return pl.pallas_call(
        attention_kernel,
        name="attention",
        out_shape=(jax.ShapeDtypeStruct((PEERS, RUN, UNIT), BF16), narrow, narrow),
        in_specs=[pl.BlockSpec(memory_space=pltpu.SMEM)] * 2 + [pl.BlockSpec(memory_space=pltpu.VMEM)] * 4,
        out_specs=[pl.BlockSpec(memory_space=pltpu.VMEM)] * 3,
        scratch_shapes=[
            pltpu.SMEM((GROUP_BLOCKS,), jnp.int32),
            pltpu.SMEM((GROUP_BLOCKS,), jnp.int32),
            pltpu.SMEM((PLANE_BLOCKS + 1,), jnp.int32),
            pltpu.SMEM((PLANE_BLOCKS + 1,), jnp.int32),
            pltpu.SMEM((DOCS,), jnp.int32),
            pltpu.VMEM((GROUP_TOKENS, HEAD_DIM), BF16),
            pltpu.VMEM((GROUP_TOKENS, HEAD_DIM), BF16),
            pltpu.VMEM((TILES, TILE_ROWS, HEAD_DIM), BF16),
            pltpu.VMEM((TILES, TILE_ROWS, HEAD_DIM), BF16),
            pltpu.VMEM((TILES, 8, TILE_ROWS), jnp.int32),
            pltpu.SMEM((2 * TILES,), jnp.int32),
            pltpu.VMEM((CHUNKS, HEAD_DIM, CHUNK), BF16),
            pltpu.VMEM((GROUP_TOKENS, HEAD_DIM), F32),
            pltpu.VMEM((GROUP_TOKENS, HEAD_DIM), F32),
            pltpu.VMEM((TILES, HEAD_DIM, TILE_ROWS), F32),
            pltpu.VMEM((PLANE_BLOCKS * BLOCK_ROWS, UNIT), F32),
            pltpu.VMEM((CHUNKS, CHUNK, TILE_ROWS), F32),
            pltpu.VMEM((CHUNKS, CHUNK, TILE_ROWS), F32),
            pltpu.VMEM((CHUNKS, 8, TILE_ROWS), F32),
        ],
        compiler_params=pltpu.CompilerParams(vmem_limit_bytes=34 * 1024 * 1024),
    )(block_target, doc_lengths, queries, grads, keys, values)


def collect_kernel(
    dq_ref,
    dk_ref,
    dv_ref,
    dq_out,
    dk_out,
    dv_out,
    inbox,
    total,
    send_sem,
    recv_sem,
    own_sem,
    ring_send,
    ring_recv,
):
    group, head, plane = place()
    me = group * KV_HEADS + head
    greet(group, head, plane)
    here = device_of(group, head, plane)
    parts = (dk_ref, dv_ref)
    outs = (dk_out, dv_out)

    def home_of(ref, width):
        return ref.at[
            pl.ds(pl.multiple_of(group * RUN, RUN), RUN), pl.ds(pl.multiple_of(head * width, width), width)
        ]

    def owner_of(slot):
        peer = lax.rem(me + PEERS - slot, PEERS)
        return device_of(peer // KV_HEADS, lax.rem(peer, KV_HEADS), plane)

    def send_wide(slot, carry):
        remote(dq_ref.at[slot], home_of(dq_out, UNIT), send_sem.at[2], recv_sem.at[2], owner_of(slot)).start()
        return carry

    def ring(way, step, n, part, src):
        target = lax.rem(plane + (1 if way == 0 else PLANES - 1), PLANES)
        return remote(
            src,
            inbox.at[way, n, step, pl.ds(part * PART, PART)],
            ring_send.at[way, n],
            ring_recv.at[way, step, n, part],
            device_of(group, head, target),
        )

    def chunk_at(way, step):
        distance = 4 - step
        return lax.rem(plane + (distance if way == 0 else PLANES - distance), PLANES)

    for step in range(4):
        for part in range(PARTS):
            piece = pl.ds(part * PART, PART)
            for n in range(2):
                for way in range(2):
                    chunk = chunk_at(way, step)
                    if step == 0 and n != way:
                        continue
                    if step == 0 or (step == 1 and n != way):
                        ring(way, step, n, part, parts[n].at[chunk, piece]).start()
                    else:
                        held = inbox.at[way, n, step - 1, piece]
                        ring(way, step - 1, n, part, held).wait_recv()
                        held[...] = (held[...].astype(F32) + parts[n][chunk, piece].astype(F32)).astype(BF16)
                        ring(way, step, n, part, held).start()
        if step == 0:
            own_wide = pltpu.make_async_copy(dq_ref.at[0], home_of(dq_out, UNIT), own_sem.at[2])
            own_wide.start()
            lax.fori_loop(1, PEERS, send_wide, 0)
    own = [pltpu.make_async_copy(total.at[n, 0], home_of(outs[n], HEAD_DIM), own_sem.at[n]) for n in range(2)]
    for part in range(PARTS):
        piece = pl.ds(part * PART, PART)
        for n in range(2):
            for way in range(2):
                ring(way, 3, n, part, inbox.at[way, n, 3, piece]).wait_recv()
            total[n, piece] = (
                parts[n][plane, piece].astype(F32)
                + inbox[0, n, 3, piece].astype(F32)
                + inbox[1, n, 3, piece].astype(F32)
            ).astype(BF16)

            def send_narrow(slot, carry):
                remote(
                    total.at[n, slot], home_of(outs[n], HEAD_DIM), send_sem.at[n], recv_sem.at[n], owner_of(slot)
                ).start()
                return carry

            if part == 0:
                own[n].start()
            lax.fori_loop(max(1, part * PART), (part + 1) * PART, send_narrow, 0)
    for way in range(2):
        for n in range(2):
            sent = inbox.at[way, n, pl.ds(0, 4 if n == way else 3)]
            remote(sent, sent, ring_send.at[way, n], ring_recv.at[way, 0, n, 0], here).wait_send()
    own_wide.wait()
    sent = dq_ref.at[pl.ds(0, PEERS - 1)]
    rest = remote(sent, sent, send_sem.at[2], recv_sem.at[2], here)
    rest.wait_send()
    rest.wait_recv()
    for n in range(2):
        sent = total.at[n, pl.ds(0, PEERS - 1)]
        rest = remote(sent, sent, send_sem.at[n], recv_sem.at[n], here)
        rest.wait_send()
        rest.wait_recv()
        own[n].wait()


def collect(dq, dk, dv):
    return pl.pallas_call(
        collect_kernel,
        name="collect",
        out_shape=(
            jax.ShapeDtypeStruct((GROUPS * RUN, KV_HEADS * UNIT), BF16),
            jax.ShapeDtypeStruct((GROUPS * RUN, KV_HEADS * HEAD_DIM), BF16),
            jax.ShapeDtypeStruct((GROUPS * RUN, KV_HEADS * HEAD_DIM), BF16),
        ),
        in_specs=[
            pl.BlockSpec(memory_space=pl.ANY),
            pl.BlockSpec(memory_space=pltpu.VMEM),
            pl.BlockSpec(memory_space=pltpu.VMEM),
        ],
        out_specs=[pl.BlockSpec(memory_space=pl.ANY)] * 3,
        scratch_shapes=[
            pltpu.VMEM((2, 2, 4, PEERS, RUN, HEAD_DIM), BF16),
            pltpu.VMEM((2, PEERS, RUN, HEAD_DIM), BF16),
            pltpu.SemaphoreType.DMA((3,)),
            pltpu.SemaphoreType.DMA((3,)),
            pltpu.SemaphoreType.DMA((3,)),
            pltpu.SemaphoreType.DMA((2, 2)),
            pltpu.SemaphoreType.DMA((2, 4, 2, PARTS)),
        ],
        compiler_params=pltpu.CompilerParams(
            collective_id=1, has_side_effects=True, vmem_limit_bytes=12 * 1024 * 1024
        ),
    )(dq, dk, dv)


def on_device(query_rows, key_rows, value_rows, output_grad, block_target, doc_lengths):
    queries, grads, keys, values = scatter(query_rows, output_grad, key_rows, value_rows)
    pairs = (GROUP_BLOCKS // 2, RUN, HEAD_DIM)
    dq, dk, dv = attention(block_target, doc_lengths, queries, grads, keys.reshape(pairs), values.reshape(pairs))
    planes = (PLANES, PEERS, RUN, HEAD_DIM)
    return collect(dq, dk.reshape(planes), dv.reshape(planes))


def solution(mesh):
    in_specs = (
        P(("grp", "ctx"), None),
        P(("grp", "ctx"), None),
        P(("grp", "ctx"), None),
        P(("grp", "ctx"), None),
        P(),
        P("grp", None),
    )
    out_specs = (P(("grp", "ctx"), None), P(("grp", "ctx"), None), P(("grp", "ctx"), None))
    return jax.shard_map(
        on_device, mesh=mesh, in_specs=in_specs, out_specs=out_specs, check_vma=False
    )
```

time: 122 us -> 105 us (0.86)
  Pallas kernels: 114 us -> 96.7 us
    pallas_call x1, Pallas kernels: 45.3 us -> 36.6 us  [collect(): pl.pallas_call(collect_kernel, name='collect', out_shape=(jax.ShapeDtypeS...]
    pallas_call x1, Pallas kernels: 25.5 us -> 20.8 us  [attention(): pl.pallas_call(attention_kernel, name='attention', out_shape=(jax.ShapeDt...]
    pallas_call x1, Pallas kernels: 42.9 us -> 39.4 us  [scatter(): pl.pallas_call(scatter_kernel, name='scatter', out_shape=(wide, wide, nar...]
    unnamed x12 -> x14, local copies, waits for them, and re-layouts: 6.25 us -> 7.25 us
where the time goes in v2:
time: 105 us
  Pallas kernels  96.7 us (92%)
  local copies, waits for them, and re-layouts  7.25 us (7%)
    pallas_call x1, Pallas kernels, scatter(): pl.pallas_call(scatter_kernel, name='scatter', out_shape=(wide, wide, nar...  39.4 us
    pallas_call x1, Pallas kernels, collect(): pl.pallas_call(collect_kernel, name='collect', out_shape=(jax.ShapeDtypeS...  36.6 us
    pallas_call x1, Pallas kernels, attention(): pl.pallas_call(attention_kernel, name='attention', out_shape=(jax.ShapeDt...  20.8 us
    unnamed x14, local copies, waits for them, and re-layouts  7.25 us

profile of v2, /device:TPU:1, one launch (start us, length us, event | category | flops | bytes accessed | tf_op | source)
XLA Modules:
  0.0 104.7 jit_solution(13286430599671431424)
XLA Ops:
  0.6 0.0 copy-start.2
  0.6 1.0 copy.9.target_ref
  1.6 0.0 copy-done.2
  1.6 0.0 copy-start
  1.6 1.2 %copy-done = bf16[128,4096]{1,0:T(8,128)(2,1)S(1)} copy-done((bf16[128,4096]{1,0:T(8,128)(2,1)S(1)}, bf16[128,4096]{1,0:T(8,128)(2,1)}, u32[]{:S(2)}) %copy-start) | copy-done | bytes 1048600
  2.8 0.0 copy-start.1
  2.9 1.2 %copy-done.1 = bf16[128,4096]{1,0:T(8,128)(2,1)S(1)} copy-done((bf16[128,4096]{1,0:T(8,128)(2,1)S(1)}, bf16[128,4096]{1,0:T(8,128)(2,1)}, u32[]{:S(2)}) %copy-start.1) | copy-done | bytes 1048600
  4.1 0.0 copy-start.3
  4.1 0.9 copy-done.3
  5.0 39.4 %scatter.1 = (bf16[32,16,1024]{2,1,0:T(8,128)(2,1)S(1)}, bf16[32,16,1024]{2,1,0:T(8,128)(2,1)S(1)}, bf16[8,32,16,128]{3,2,1,0:T(8,128)(2,1)S(1)}, bf16[8,32,16,128]{3,2,1,0:T(8,128)(2,1)S(1)}) custom-call(bf16[128,4096]{1,0:T(8,128)(2,1)S(1)} %copy-done, bf16[128,4096]{1,0:T(8,128)(2,1)S(1)} %copy-done.1, bf16[128,512]{1,0:T(8,128)(2,1)S(1)} %copy-done.2, ...), custom_call_target="tpu_custom_call" | custom-call | tf_op jit(solution)/shard_map/scatter/pallas_call | solution.py:189
  44.4 0.0 copy-start.4
  44.4 0.6 copy-done.4
  45.0 20.8 %attention.1 = (bf16[32,16,1024]{2,1,0:T(8,128)(2,1)S(1)}, bf16[256,16,128]{2,1,0:T(8,128)(2,1)S(1)}, bf16[256,16,128]{2,1,0:T(8,128)(2,1)S(1)}) custom-call(s32[8,32,16]{2,1,0:T(8,128)S(1)} %copy.9.target_ref, s32[1,16]{1,0:T(1,128)S(1)} %copy-done.4, bf16[32,16,1024]{2,1,0:T(8,128)(2,1)S(1)} %get-tuple-element.10.q_ref, ...), custom_call_target="tpu_custom_call" | custom-call | tf_op jit(solution)/shard_map/attention/pallas_call | solution.py:479
  65.8 36.6 %collect.1 = (bf16[128,4096]{1,0:T(8,128)(2,1)S(1)}, bf16[128,512]{1,0:T(8,128)(2,1)S(1)}, bf16[128,512]{1,0:T(8,128)(2,1)S(1)}) custom-call(bf16[32,16,1024]{2,1,0:T(8,128)(2,1)S(1)} %get-tuple-element.14.dq_ref, bf16[8,32,16,128]{3,2,1,0:T(8,128)(2,1)S(1)} %bitcast.4, bf16[8,32,16,128]{3,2,1,0:T(8,128)(2,1)S(1)} %bitcast.5), custom_call_target="tpu_custom_call" | custom-call | tf_op jit(solution)/shard_map/collect/pallas_call | solution.py:617
  102.4 1.0 copy.13
  103.4 0.7 copy.14
  104.0 0.7 copy.15
Async XLA Ops:
  0.6 1.0 copy-start.2
  1.6 1.2 %copy-start = (bf16[128,4096]{1,0:T(8,128)(2,1)S(1)}, bf16[128,4096]{1,0:T(8,128)(2,1)}, u32[]{:S(2)}) copy-start(bf16[128,4096]{1,0:T(8,128)(2,1)} %q_ref.1) | copy-start | bytes 3145732
  2.8 1.2 %copy-start.1 = (bf16[128,4096]{1,0:T(8,128)(2,1)S(1)}, bf16[128,4096]{1,0:T(8,128)(2,1)}, u32[]{:S(2)}) copy-start(bf16[128,4096]{1,0:T(8,128)(2,1)} %g_ref.1) | copy-start | bytes 3145732
  4.1 0.9 copy-start.3
  44.4 0.7 copy-start.4

commit v3 on v2

--- a/solution.py
+++ b/solution.py
@@ -82,7 +82,24 @@
 
 
 def scatter_kernel(
-    q_ref, g_ref, k_ref, v_ref, q_out, g_out, k_out, v_out, send_sem, narrow_recv, wide_recv, own_sem, ring_send, ring_recv
+    q_ref,
+    g_ref,
+    k_ref,
+    v_ref,
+    target_ref,
+    length_ref,
+    q_out,
+    g_out,
+    k_out,
+    v_out,
+    target_out,
+    length_out,
+    send_sem,
+    narrow_recv,
+    wide_recv,
+    own_sem,
+    ring_send,
+    ring_recv,
 ):
     group, head, plane = place()
     me = group * KV_HEADS + head
@@ -130,11 +147,15 @@
         pltpu.make_async_copy(run_of(src, group, head, UNIT), dst.at[0], own_sem.at[2 + n])
         for n, (src, dst) in enumerate(wide)
     ]
+    own += [
+        pltpu.make_async_copy(target_ref, target_out, own_sem.at[4]),
+        pltpu.make_async_copy(length_ref, length_out, own_sem.at[5]),
+    ]
     own[0].start()
     own[1].start()
     lax.fori_loop(1, PEERS, send_narrow, 0)
-    own[2].start()
-    own[3].start()
+    for copy in own[2:]:
+        copy.start()
 
     def ring(way, step, n, part):
         chunk = lax.rem(plane + (PLANES - step if way == 0 else step), PLANES)
@@ -173,6 +194,8 @@
         for n in range(2):
             sent = narrow[n][1].at[pl.ds(0, 4 if n == way else 3)]
             remote(sent, sent, ring_send.at[way, n], ring_recv.at[way, 0, n, 0], here).wait_send()
+    own[4].wait()
+    own[5].wait()
     for n in range(2):
         sent = narrow[n][1].at[0, pl.ds(0, PEERS - 1)]
         remote(sent, sent, send_sem.at[n], narrow_recv.at[n, 0], here).wait_send()
@@ -183,27 +206,39 @@
         rest.wait_send()
 
 
-def scatter(query_rows, output_grad, key_rows, value_rows):
+def scatter(query_rows, output_grad, key_rows, value_rows, block_target, doc_lengths):
     wide = jax.ShapeDtypeStruct((PEERS, RUN, UNIT), BF16)
     narrow = jax.ShapeDtypeStruct((PLANES, PEERS, RUN, HEAD_DIM), BF16)
     return pl.pallas_call(
         scatter_kernel,
         name="scatter",
-        out_shape=(wide, wide, narrow, narrow),
-        in_specs=[pl.BlockSpec(memory_space=pl.ANY)] * 4,
-        out_specs=[pl.BlockSpec(memory_space=pl.ANY)] * 4,
+        out_shape=(
+            wide,
+            wide,
+            narrow,
+            narrow,
+            jax.ShapeDtypeStruct(block_target.shape, jnp.int32),
+            jax.ShapeDtypeStruct(doc_lengths.shape, jnp.int32),
+        ),
+        in_specs=[pl.BlockSpec(memory_space=pltpu.HBM)] * 6,
+        out_specs=[pl.BlockSpec(memory_space=pl.ANY)] * 4 + [pl.BlockSpec(memory_space=pltpu.SMEM)] * 2,
         scratch_shapes=[
             pltpu.SemaphoreType.DMA((4,)),
             pltpu.SemaphoreType.DMA((2, PARTS)),
             pltpu.SemaphoreType.DMA((2,)),
-            pltpu.SemaphoreType.DMA((4,)),
+            pltpu.SemaphoreType.DMA((6,)),
             pltpu.SemaphoreType.DMA((2, 2)),
             pltpu.SemaphoreType.DMA((2, 4, 2, PARTS)),
         ],
         compiler_params=pltpu.CompilerParams(
             collective_id=0, has_side_effects=True, vmem_limit_bytes=2 * 1024 * 1024
         ),
-    )(query_rows, output_grad, key_rows, value_rows)
+    )(
+        *(
+            pltpu.with_memory_space_constraint(rows, pltpu.HBM)
+            for rows in (query_rows, output_grad, key_rows, value_rows, block_target, doc_lengths)
+        )
+    )
 
 
 def attention_kernel(
@@ -245,7 +280,7 @@
 
     def target_of(source, from_plane, which):
         ctx = ((source >> 1) & 1) * 16 + (source & 1) + from_plane * 2
-        return target_ref[source >> 2, ctx, 2 * group + which] - group * GROUP_BLOCKS
+        return target_ref[source >> 2, 2 * group + which, ctx] - group * GROUP_BLOCKS
 
     def clear(step, carry):
         holder[step] = 0
@@ -643,12 +678,34 @@
     )(dq, dk, dv)
 
 
+def deliver_kernel(*refs):
+    copies = [pltpu.make_async_copy(refs[n], refs[3 + n], refs[6].at[n]) for n in range(3)]
+    for copy in copies:
+        copy.start()
+    for copy in copies:
+        copy.wait()
+
+
+def deliver(*grads):
+    return pl.pallas_call(
+        deliver_kernel,
+        name="deliver",
+        out_shape=tuple(jax.ShapeDtypeStruct(grad.shape, grad.dtype) for grad in grads),
+        in_specs=[pl.BlockSpec(memory_space=pl.ANY)] * 3,
+        out_specs=[pl.BlockSpec(memory_space=pl.ANY)] * 3,
+        scratch_shapes=[pltpu.SemaphoreType.DMA((3,))],
+        compiler_params=pltpu.CompilerParams(vmem_limit_bytes=1024 * 1024),
+    )(*grads)
+
+
 def on_device(query_rows, key_rows, value_rows, output_grad, block_target, doc_lengths):
-    queries, grads, keys, values = scatter(query_rows, output_grad, key_rows, value_rows)
+    queries, grads, keys, values, targets, lengths = scatter(
+        query_rows, output_grad, key_rows, value_rows, block_target.transpose(0, 2, 1), doc_lengths
+    )
     pairs = (GROUP_BLOCKS // 2, RUN, HEAD_DIM)
-    dq, dk, dv = attention(block_target, doc_lengths, queries, grads, keys.reshape(pairs), values.reshape(pairs))
+    dq, dk, dv = attention(targets, lengths, queries, grads, keys.reshape(pairs), values.reshape(pairs))
     planes = (PLANES, PEERS, RUN, HEAD_DIM)
-    return collect(dq, dk.reshape(planes), dv.reshape(planes))
+    return deliver(*collect(dq, dk.reshape(planes), dv.reshape(planes)))
 
 
 def solution(mesh):

time: 105 us -> 100 us (0.952)
  local copies, waits for them, and re-layouts: 7.25 us -> 0 us
  Pallas kernels: 96.7 us -> 99.5 us
    unnamed x14 -> x0, local copies, waits for them, and re-layouts: 7.25 us -> none
    pallas_call x1, Pallas kernels: 39.4 us -> 42.3 us  [scatter(): pl.pallas_call(scatter_kernel, name='scatter', out_shape=(wide, wide, nar...]
    pallas_call x1, Pallas kernels: 20.8 us -> 19.6 us  [attention(): pl.pallas_call(attention_kernel, name='attention', out_shape=(jax.ShapeDt...]
    pallas_call x0 -> x1, Pallas kernels: none -> 1.07 us  [deliver(): pl.pallas_call(deliver_kernel, name='deliver', out_shape=tuple((jax.Shape...]
where the time goes in v3:
time: 100 us
  Pallas kernels  99.5 us (100%)
    pallas_call x1, Pallas kernels, scatter(): pl.pallas_call(scatter_kernel, name='scatter', out_shape=(wide, wide, nar...  42.3 us
    pallas_call x1, Pallas kernels, collect(): pl.pallas_call(collect_kernel, name='collect', out_shape=(jax.ShapeDtypeS...  36.5 us
    pallas_call x1, Pallas kernels, attention(): pl.pallas_call(attention_kernel, name='attention', out_shape=(jax.ShapeDt...  19.6 us

profile of v3, /device:TPU:1, one launch (start us, length us, event | category | flops | bytes accessed | tf_op | source)
XLA Modules:
  0.0 100.1 jit_solution(16022435953389832503)
XLA Ops:
  0.6 42.3 %scatter.1 = (bf16[32,16,1024]{2,1,0:T(8,128)(2,1)S(1)}, bf16[32,16,1024]{2,1,0:T(8,128)(2,1)S(1)}, bf16[8,32,16,128]{3,2,1,0:T(8,128)(2,1)S(1)}, bf16[8,32,16,1...) custom-call(bf16[128,4096]{1,0:T(8,128)(2,1)} %q_ref.1, bf16[128,4096]{1,0:T(8,128)(2,1)} %g_ref.1, ...), custom_call_target="tpu_custom_call" | custom-call | tf_op jit(solution)/shard_map/scatter/pallas_call | solution.py:212
  43.0 19.6 %attention.1 = (bf16[32,16,1024]{2,1,0:T(8,128)(2,1)S(1)}, bf16[256,16,128]{2,1,0:T(8,128)(2,1)S(1)}, bf16[256,16,128]{2,1,0:T(8,128)(2,1)S(1)}) custom-call(s32[8,16,32]{2,1,0:T(8,128)S(1)} %get-tuple-element.15.target_ref, s32[1,16]{1,0:T(1,128)S(1)} %get-tuple-element.16.length_ref, bf16[32,16,1024]{2,1,0:T(8,128)(2,1)S(1)} %get-tuple-element.17.q_ref, ...), custom_call_target="tpu_custom_call" | custom-call | tf_op jit(solution)/shard_map/attention/pallas_call | solution.py:514
  62.6 36.5 %collect.1 = (bf16[128,4096]{1,0:T(8,128)(2,1)S(1)}, bf16[128,512]{1,0:T(8,128)(2,1)S(1)}, bf16[128,512]{1,0:T(8,128)(2,1)S(1)}) custom-call(bf16[32,16,1024]{2,1,0:T(8,128)(2,1)S(1)} %get-tuple-element.21.dq_ref, bf16[8,32,16,128]{3,2,1,0:T(8,128)(2,1)S(1)} %bitcast.5, bf16[8,32,16,128]{3,2,1,0:T(8,128)(2,1)S(1)} %bitcast.6), custom_call_target="tpu_custom_call" | custom-call | tf_op jit(solution)/shard_map/collect/pallas_call | solution.py:652
  99.1 1.1 %deliver.1 = (bf16[128,4096]{1,0:T(8,128)(2,1)}, bf16[128,512]{1,0:T(8,128)(2,1)}, bf16[128,512]{1,0:T(8,128)(2,1)}) custom-call(bf16[128,4096]{1,0:T(8,128)(2,1)S(1)} %get-tuple-element.24.refs_0_, bf16[128,512]{1,0:T(8,128)(2,1)S(1)} %get-tuple-element.25.refs_1_, bf16[128,512]{1,0:T(8,128)(2,1)S(1)} %get-tuple-element.26.refs_2_), custom_call_target="tpu_custom_call" | custom-call | tf_op jit(solution)/shard_map/deliver/pallas_call | solution.py:690

commit v4 on v3

--- a/solution.py
+++ b/solution.py
@@ -20,9 +20,11 @@
 DOCS = 16
 TILE_BLOCKS = 4
 TILE_ROWS = TILE_BLOCKS * SHARE * BLOCK_ROWS
+TILE_PARTS = TILE_ROWS // BLOCK_ROWS
 TILES = PLANE_BLOCKS // TILE_BLOCKS
 CHUNK = 128
 CHUNKS = GROUP_TOKENS // CHUNK
+CHUNK_BLOCKS = CHUNK // BLOCK_ROWS
 FIXED_MAX = 7
 TOGETHER = 2
 UNROLL_PREP = 2
@@ -30,7 +32,8 @@
 EXP2_SCALE = SCORE_SCALE * 1.4426950408889634
 PARTS = 4
 PART = PEERS // PARTS
-WIDE_STEPS = (1, 32, 32, 32, 32)
+WIDE_EARLY = 4
+WIDE_EACH = 2
 MESH = pl.DeviceIdType.MESH
 F32 = jnp.float32
 BF16 = jnp.bfloat16
@@ -48,6 +51,16 @@
 
 def device_of(group, head, plane):
     return {"grp": group, "ctx": (head // 2) * 16 + plane * 2 + head % 2}
+
+
+def half_of(pair, which):
+    wide = pair.astype(F32)
+    return jnp.where(which == 0, wide[:BLOCK_ROWS], wide[BLOCK_ROWS:])
+
+
+def target_of(target_ref, group, source, from_plane, which):
+    ctx = lax.rem(lax.div(source, 2), 2) * 16 + lax.rem(source, 2) + from_plane * 2
+    return lax.rem(target_ref[lax.div(source, KV_HEADS), 2 * group + which, ctx], GROUP_BLOCKS)
 
 
 def greet(group, head, plane):
@@ -90,10 +103,16 @@
     length_ref,
     q_out,
     g_out,
+    k_pack,
+    v_pack,
+    k_turned,
+    target_out,
+    length_out,
+    ranks_out,
     k_out,
     v_out,
-    target_out,
-    length_out,
+    table,
+    packed_from,
     send_sem,
     narrow_recv,
     wide_recv,
@@ -169,8 +188,47 @@
             device_of(group, head, target),
         )
 
+    def make_tables():
+        own[4].wait()
+        own[5].wait()
+        lane = lax.broadcasted_iota(jnp.int32, (8, 128), 1)
+        place_of = lax.broadcasted_iota(jnp.int32, (8, 128), 0) * 128 + lane
+
+        def invert(source, inverse):
+            slot = lax.rem(me + PEERS - source, PEERS)
+            for from_plane in range(PLANES):
+                for which in range(2):
+                    block = target_of(target_out, group, source, from_plane, which)
+                    inverse = jnp.where(place_of == block, 2 * (from_plane * PEERS + slot) + which, inverse)
+            return inverse
+
+        table[0] = lax.fori_loop(0, PEERS, invert, jnp.zeros((8, 128), jnp.int32))
+
+        def mine(step):
+            return target_of(target_out, group, lax.rem(me + PEERS - lax.div(step, 2), PEERS), plane, lax.rem(step, 2))
+
+        blocks = lax.fori_loop(
+            0,
+            PLANE_BLOCKS,
+            lambda step, blocks: jnp.where(lane == step, mine(step), blocks),
+            jnp.full((8, 128), GROUP_BLOCKS, jnp.int32),
+            unroll=8,
+        )
+        table[1] = lax.fori_loop(
+            0,
+            PLANE_BLOCKS,
+            lambda step, rank: rank + jnp.where(blocks > mine(step), 1, 0),
+            jnp.zeros((8, 128), jnp.int32),
+            unroll=8,
+        )
+        for n, dst in enumerate((packed_from, ranks_out)):
+            copy = pltpu.make_async_copy(table.at[n], dst, own_sem.at[6 + n])
+            copy.start()
+            copy.wait()
+
+    lax.fori_loop(1, WIDE_EARLY, send_wide, 0)
+    wide_next = WIDE_EARLY
     for step in range(4):
-        lax.fori_loop(WIDE_STEPS[step], WIDE_STEPS[step + 1], send_wide, 0)
         for part in range(PARTS):
             for n in range(2):
                 if step == 0:
@@ -184,6 +242,11 @@
                     if step > 0:
                         ring(way, step - 1, n, part).wait_recv()
                     ring(way, step, n, part).start()
+                wide_after = min(wide_next + WIDE_EACH, PEERS)
+                lax.fori_loop(wide_next, wide_after, send_wide, 0)
+                wide_next = wide_after
+        if step == 1:
+            make_tables()
     for part in range(PARTS):
         for way in range(2):
             ring(way, 2, 1 - way, part).wait_recv()
@@ -194,8 +257,19 @@
         for n in range(2):
             sent = narrow[n][1].at[pl.ds(0, 4 if n == way else 3)]
             remote(sent, sent, ring_send.at[way, n], ring_recv.at[way, 0, n, 0], here).wait_send()
-    own[4].wait()
-    own[5].wait()
+
+    def pack(chunk, carry):
+        first = chunk * CHUNK_BLOCKS
+        rows = pl.ds(pl.multiple_of(chunk * CHUNK, CHUNK), CHUNK)
+        held = [packed_from[lax.div(first + n, 128), lax.rem(first + n, 128)] for n in range(CHUNK_BLOCKS)]
+        keys = jnp.concatenate([half_of(k_out[h >> 6, (h >> 1) & (PEERS - 1)], h & 1) for h in held], axis=0)
+        k_pack[rows, :] = keys.astype(BF16)
+        k_turned[chunk] = jnp.transpose(keys).astype(BF16)
+        values = jnp.concatenate([half_of(v_out[h >> 6, (h >> 1) & (PEERS - 1)], h & 1) for h in held], axis=0)
+        v_pack[rows, :] = values.astype(BF16)
+        return carry
+
+    lax.fori_loop(0, CHUNKS, pack, 0)
     for n in range(2):
         sent = narrow[n][1].at[0, pl.ds(0, PEERS - 1)]
         remote(sent, sent, send_sem.at[n], narrow_recv.at[n, 0], here).wait_send()
@@ -208,30 +282,39 @@
 
 def scatter(query_rows, output_grad, key_rows, value_rows, block_target, doc_lengths):
     wide = jax.ShapeDtypeStruct((PEERS, RUN, UNIT), BF16)
-    narrow = jax.ShapeDtypeStruct((PLANES, PEERS, RUN, HEAD_DIM), BF16)
+    narrow = pltpu.VMEM((PLANES, PEERS, RUN, HEAD_DIM), BF16)
+    packed = jax.ShapeDtypeStruct((GROUP_TOKENS, HEAD_DIM), BF16)
     return pl.pallas_call(
         scatter_kernel,
         name="scatter",
         out_shape=(
             wide,
             wide,
+            packed,
+            packed,
+            jax.ShapeDtypeStruct((CHUNKS, HEAD_DIM, CHUNK), BF16),
+            jax.ShapeDtypeStruct(block_target.shape, jnp.int32),
+            jax.ShapeDtypeStruct(doc_lengths.shape, jnp.int32),
+            jax.ShapeDtypeStruct((8, 128), jnp.int32),
+        ),
+        in_specs=[pl.BlockSpec(memory_space=pltpu.HBM)] * 6,
+        out_specs=[pl.BlockSpec(memory_space=pl.ANY)] * 2
+        + [pl.BlockSpec(memory_space=pltpu.VMEM)] * 3
+        + [pl.BlockSpec(memory_space=pltpu.SMEM)] * 3,
+        scratch_shapes=[
             narrow,
             narrow,
-            jax.ShapeDtypeStruct(block_target.shape, jnp.int32),
-            jax.ShapeDtypeStruct(doc_lengths.shape, jnp.int32),
-        ),
-        in_specs=[pl.BlockSpec(memory_space=pltpu.HBM)] * 6,
-        out_specs=[pl.BlockSpec(memory_space=pl.ANY)] * 4 + [pl.BlockSpec(memory_space=pltpu.SMEM)] * 2,
-        scratch_shapes=[
+            pltpu.VMEM((2, 8, 128), jnp.int32),
+            pltpu.SMEM((8, 128), jnp.int32),
             pltpu.SemaphoreType.DMA((4,)),
             pltpu.SemaphoreType.DMA((2, PARTS)),
             pltpu.SemaphoreType.DMA((2,)),
-            pltpu.SemaphoreType.DMA((6,)),
+            pltpu.SemaphoreType.DMA((8,)),
             pltpu.SemaphoreType.DMA((2, 2)),
             pltpu.SemaphoreType.DMA((2, 4, 2, PARTS)),
         ],
         compiler_params=pltpu.CompilerParams(
-            collective_id=0, has_side_effects=True, vmem_limit_bytes=2 * 1024 * 1024
+            collective_id=0, has_side_effects=True, vmem_limit_bytes=10 * 1024 * 1024
         ),
     )(
         *(
@@ -242,98 +325,51 @@
 
 
 def attention_kernel(
+    length_ref,
+    rank_ref,
     target_ref,
-    length_ref,
     q_ref,
     g_ref,
-    k_ref,
-    v_ref,
-    dq_ref,
-    dk_ref,
-    dv_ref,
-    packed_to,
-    holder,
+    k_pack,
+    v_pack,
+    k_turned,
+    dq_turned,
+    dk_acc,
+    dv_acc,
     query_order,
     query_block,
     doc_ends,
-    k_pack,
-    v_pack,
     q_tiles,
     g_tiles,
     bounds,
     spans,
-    k_turned,
-    dk_acc,
-    dv_acc,
-    dq_turned,
-    dq_acc,
     exps,
     probs,
     maxes,
 ):
-    def half_of(pair, which):
-        wide = pair.astype(F32)
-        return jnp.where(which == 0, wide[:BLOCK_ROWS], wide[BLOCK_ROWS:])
-
     group, head, plane = place()
     me = group * KV_HEADS + head
 
-    def target_of(source, from_plane, which):
-        ctx = ((source >> 1) & 1) * 16 + (source & 1) + from_plane * 2
-        return target_ref[source >> 2, 2 * group + which, ctx] - group * GROUP_BLOCKS
-
-    def clear(step, carry):
-        holder[step] = 0
-        return carry
-
-    lax.fori_loop(0, GROUP_BLOCKS, clear, 0, unroll=16)
-
-    def hold(slot, carry):
-        for which in range(2):
-            holder[target_of((me - slot) & (PEERS - 1), plane, which)] = 2 * slot + which + 1
-        return carry
-
-    lax.fori_loop(0, PEERS, hold, 0, unroll=4)
+    def sort(step, carry):
+        rank = rank_ref[0, step]
+        query_order[rank] = step
+        query_block[rank] = target_of(target_ref, group, lax.rem(me + PEERS - lax.div(step, 2), PEERS), plane, lax.rem(step, 2))
+        return carry
+
+    lax.fori_loop(0, PLANE_BLOCKS, sort, 0, unroll=8)
 
     end = jnp.int32(0)
     for n in range(DOCS):
         end = end + length_ref[0, n]
         doc_ends[n] = end
 
-    def pack(source, carry):
-        slot = (me - source) & (PEERS - 1)
-        for from_plane in range(PLANES):
-            pair = from_plane * PEERS + slot
-            keys = k_ref[pair].astype(F32)
-            values = v_ref[pair].astype(F32)
-            for which in range(2):
-                block = target_of(source, from_plane, which)
-                packed_to[2 * pair + which] = block
-                rows = pl.ds(pl.multiple_of(block * BLOCK_ROWS, BLOCK_ROWS), BLOCK_ROWS)
-                half = slice(which * BLOCK_ROWS, (which + 1) * BLOCK_ROWS)
-                dk_acc[rows, :] = keys[half]
-                dv_acc[rows, :] = values[half]
-        return carry
-
-    lax.fori_loop(0, PEERS, pack, 0, unroll=2)
-
-    def turn(step, found):
+    def clear(step, carry):
         rows = pl.ds(pl.multiple_of(step * CHUNK, CHUNK), CHUNK)
-        keys = dk_acc[rows, :]
-        k_pack[rows, :] = keys.astype(BF16)
-        k_turned[step] = jnp.transpose(keys).astype(BF16)
-        v_pack[rows, :] = dv_acc[rows, :].astype(BF16)
         dk_acc[rows, :] = jnp.zeros((CHUNK, HEAD_DIM), F32)
         dv_acc[rows, :] = jnp.zeros((CHUNK, HEAD_DIM), F32)
-        for n in range(CHUNK // BLOCK_ROWS):
-            block = step * (CHUNK // BLOCK_ROWS) + n
-            slot = holder[block]
-            query_order[found] = slot - 1
-            query_block[found] = block
-            found = found + jnp.where(slot > 0, 1, 0)
-        return found
-
-    lax.fori_loop(0, CHUNKS, turn, jnp.int32(0), unroll=2)
+        return carry
+
+    lax.fori_loop(0, CHUNKS, clear, 0, unroll=2)
 
     lane = lax.broadcasted_iota(jnp.int32, (1, TILE_ROWS), 1)
     owner = lane // (SHARE * BLOCK_ROWS)
@@ -481,74 +517,43 @@
 
     lax.fori_loop(0, TILES // TOGETHER, query_tiles, 0)
 
-    def place_queries(tile, carry):
-        dq = jnp.transpose(dq_turned[tile]) * SCORE_SCALE
-        for n in range(TILE_BLOCKS):
-            rows = pl.ds(pl.multiple_of(query_order[tile * TILE_BLOCKS + n] * BLOCK_ROWS, BLOCK_ROWS), BLOCK_ROWS)
-            for h in range(SHARE):
-                part = (n * SHARE + h) * BLOCK_ROWS
-                dq_acc[rows, h * HEAD_DIM : (h + 1) * HEAD_DIM] = dq[part : part + BLOCK_ROWS]
-        return carry
-
-    lax.fori_loop(0, TILES, place_queries, 0, unroll=UNROLL_PREP)
-
-    def finish_queries(step, carry):
-        dq_ref[step] = dq_acc[pl.ds(pl.multiple_of(step * RUN, RUN), RUN), :].astype(BF16)
-        return carry
-
-    lax.fori_loop(0, PEERS, finish_queries, 0, unroll=2)
-
-    def finish_keys(step, carry):
-        first = pl.multiple_of(packed_to[2 * step] * BLOCK_ROWS, BLOCK_ROWS)
-        second = pl.multiple_of(packed_to[2 * step + 1] * BLOCK_ROWS, BLOCK_ROWS)
-        for src, dst, scale in ((dk_acc, dk_ref, SCORE_SCALE), (dv_acc, dv_ref, 1.0)):
-            rows = jnp.concatenate([src[pl.ds(first, BLOCK_ROWS), :], src[pl.ds(second, BLOCK_ROWS), :]], axis=0)
-            dst[step] = (rows * scale).astype(BF16)
-        return carry
-
-    lax.fori_loop(0, GROUP_BLOCKS // 2, finish_keys, 0, unroll=8)
-
-
-def attention(block_target, doc_lengths, queries, grads, keys, values):
-    narrow = jax.ShapeDtypeStruct((GROUP_BLOCKS // 2, RUN, HEAD_DIM), BF16)
+
+def attention(doc_lengths, ranks, block_target, queries, grads, keys, values, keys_turned):
+    acc = jax.ShapeDtypeStruct((GROUP_TOKENS, HEAD_DIM), F32)
     return pl.pallas_call(
         attention_kernel,
         name="attention",
-        out_shape=(jax.ShapeDtypeStruct((PEERS, RUN, UNIT), BF16), narrow, narrow),
-        in_specs=[pl.BlockSpec(memory_space=pltpu.SMEM)] * 2 + [pl.BlockSpec(memory_space=pltpu.VMEM)] * 4,
+        out_shape=(jax.ShapeDtypeStruct((TILES, HEAD_DIM, TILE_ROWS), F32), acc, acc),
+        in_specs=[pl.BlockSpec(memory_space=pltpu.SMEM)] * 3 + [pl.BlockSpec(memory_space=pltpu.VMEM)] * 5,
         out_specs=[pl.BlockSpec(memory_space=pltpu.VMEM)] * 3,
         scratch_shapes=[
-            pltpu.SMEM((GROUP_BLOCKS,), jnp.int32),
-            pltpu.SMEM((GROUP_BLOCKS,), jnp.int32),
-            pltpu.SMEM((PLANE_BLOCKS + 1,), jnp.int32),
-            pltpu.SMEM((PLANE_BLOCKS + 1,), jnp.int32),
+            pltpu.SMEM((PLANE_BLOCKS,), jnp.int32),
+            pltpu.SMEM((PLANE_BLOCKS,), jnp.int32),
             pltpu.SMEM((DOCS,), jnp.int32),
-            pltpu.VMEM((GROUP_TOKENS, HEAD_DIM), BF16),
-            pltpu.VMEM((GROUP_TOKENS, HEAD_DIM), BF16),
             pltpu.VMEM((TILES, TILE_ROWS, HEAD_DIM), BF16),
             pltpu.VMEM((TILES, TILE_ROWS, HEAD_DIM), BF16),
             pltpu.VMEM((TILES, 8, TILE_ROWS), jnp.int32),
             pltpu.SMEM((2 * TILES,), jnp.int32),
-            pltpu.VMEM((CHUNKS, HEAD_DIM, CHUNK), BF16),
-            pltpu.VMEM((GROUP_TOKENS, HEAD_DIM), F32),
-            pltpu.VMEM((GROUP_TOKENS, HEAD_DIM), F32),
-            pltpu.VMEM((TILES, HEAD_DIM, TILE_ROWS), F32),
-            pltpu.VMEM((PLANE_BLOCKS * BLOCK_ROWS, UNIT), F32),
             pltpu.VMEM((CHUNKS, CHUNK, TILE_ROWS), F32),
             pltpu.VMEM((CHUNKS, CHUNK, TILE_ROWS), F32),
             pltpu.VMEM((CHUNKS, 8, TILE_ROWS), F32),
         ],
-        compiler_params=pltpu.CompilerParams(vmem_limit_bytes=34 * 1024 * 1024),
-    )(block_target, doc_lengths, queries, grads, keys, values)
+        compiler_params=pltpu.CompilerParams(vmem_limit_bytes=30 * 1024 * 1024),
+    )(doc_lengths, ranks, block_target, queries, grads, keys, values, keys_turned)
 
 
 def collect_kernel(
-    dq_ref,
+    rank_ref,
+    target_ref,
+    dq_turned,
     dk_ref,
     dv_ref,
     dq_out,
     dk_out,
     dv_out,
+    dq_ref,
+    dq_tiles,
+    outbox,
     inbox,
     total,
     send_sem,
@@ -573,7 +578,28 @@
         peer = lax.rem(me + PEERS - slot, PEERS)
         return device_of(peer // KV_HEADS, lax.rem(peer, KV_HEADS), plane)
 
+    def rows_of(n, slot, chunk):
+        halves = []
+        for which in range(2):
+            block = target_of(target_ref, group, lax.rem(me + PEERS - slot, PEERS), chunk, which)
+            halves.append(parts[n][block])
+        rows = jnp.concatenate(halves, axis=0)
+        return rows * SCORE_SCALE if n == 0 else rows
+
+    def turn(tile, carry):
+        rows = jnp.transpose(dq_turned[tile]) * SCORE_SCALE
+        dq_tiles[pl.ds(tile * TILE_PARTS, TILE_PARTS)] = rows.reshape(TILE_PARTS, BLOCK_ROWS, HEAD_DIM)
+        return carry
+
+    def put_wide(slot):
+        halves = []
+        for which in range(2):
+            first = rank_ref[0, 2 * slot + which] * SHARE
+            halves.append(jnp.concatenate([dq_tiles[first + h] for h in range(SHARE)], axis=1))
+        dq_ref[slot] = jnp.concatenate(halves, axis=0).astype(BF16)
+
     def send_wide(slot, carry):
+        put_wide(slot)
         remote(dq_ref.at[slot], home_of(dq_out, UNIT), send_sem.at[2], recv_sem.at[2], owner_of(slot)).start()
         return carry
 
@@ -600,27 +626,48 @@
                     if step == 0 and n != way:
                         continue
                     if step == 0 or (step == 1 and n != way):
-                        ring(way, step, n, part, parts[n].at[chunk, piece]).start()
+
+                        def fill(slot, carry):
+                            outbox[way, n, slot] = rows_of(n, slot, chunk).astype(BF16)
+                            return carry
+
+                        lax.fori_loop(part * PART, (part + 1) * PART, fill, 0, unroll=4)
+                        ring(way, step, n, part, outbox.at[way, n, piece]).start()
                     else:
                         held = inbox.at[way, n, step - 1, piece]
                         ring(way, step - 1, n, part, held).wait_recv()
-                        held[...] = (held[...].astype(F32) + parts[n][chunk, piece].astype(F32)).astype(BF16)
+
+                        def add(slot, carry):
+                            sum_so_far = inbox[way, n, step - 1, slot].astype(F32)
+                            inbox[way, n, step - 1, slot] = (sum_so_far + rows_of(n, slot, chunk)).astype(BF16)
+                            return carry
+
+                        lax.fori_loop(part * PART, (part + 1) * PART, add, 0, unroll=4)
                         ring(way, step, n, part, held).start()
+                if step > 0:
+                    wide_after = min(wide_next + 2, PEERS)
+                    lax.fori_loop(wide_next, wide_after, send_wide, 0)
+                    wide_next = wide_after
         if step == 0:
+            lax.fori_loop(0, TILES, turn, 0)
+            put_wide(0)
             own_wide = pltpu.make_async_copy(dq_ref.at[0], home_of(dq_out, UNIT), own_sem.at[2])
             own_wide.start()
-            lax.fori_loop(1, PEERS, send_wide, 0)
+            lax.fori_loop(1, 4, send_wide, 0)
+            wide_next = 4
     own = [pltpu.make_async_copy(total.at[n, 0], home_of(outs[n], HEAD_DIM), own_sem.at[n]) for n in range(2)]
     for part in range(PARTS):
         piece = pl.ds(part * PART, PART)
         for n in range(2):
             for way in range(2):
                 ring(way, 3, n, part, inbox.at[way, n, 3, piece]).wait_recv()
-            total[n, piece] = (
-                parts[n][plane, piece].astype(F32)
-                + inbox[0, n, 3, piece].astype(F32)
-                + inbox[1, n, 3, piece].astype(F32)
-            ).astype(BF16)
+
+            def sum_up(slot, carry):
+                arrived = inbox[0, n, 3, slot].astype(F32) + inbox[1, n, 3, slot].astype(F32)
+                total[n, slot] = (rows_of(n, slot, plane) + arrived).astype(BF16)
+                return carry
+
+            lax.fori_loop(part * PART, (part + 1) * PART, sum_up, 0, unroll=4)
 
             def send_narrow(slot, carry):
                 remote(
@@ -648,7 +695,7 @@
         own[n].wait()
 
 
-def collect(dq, dk, dv):
+def collect(ranks, block_target, dq, dk, dv):
     return pl.pallas_call(
         collect_kernel,
         name="collect",
@@ -657,13 +704,12 @@
             jax.ShapeDtypeStruct((GROUPS * RUN, KV_HEADS * HEAD_DIM), BF16),
             jax.ShapeDtypeStruct((GROUPS * RUN, KV_HEADS * HEAD_DIM), BF16),
         ),
-        in_specs=[
-            pl.BlockSpec(memory_space=pl.ANY),
-            pl.BlockSpec(memory_space=pltpu.VMEM),
-            pl.BlockSpec(memory_space=pltpu.VMEM),
-        ],
+        in_specs=[pl.BlockSpec(memory_space=pltpu.SMEM)] * 2 + [pl.BlockSpec(memory_space=pltpu.VMEM)] * 3,
         out_specs=[pl.BlockSpec(memory_space=pl.ANY)] * 3,
         scratch_shapes=[
+            pltpu.VMEM((PEERS, RUN, UNIT), BF16),
+            pltpu.VMEM((TILES * TILE_PARTS, BLOCK_ROWS, HEAD_DIM), F32),
+            pltpu.VMEM((2, 2, PEERS, RUN, HEAD_DIM), BF16),
             pltpu.VMEM((2, 2, 4, PEERS, RUN, HEAD_DIM), BF16),
             pltpu.VMEM((2, PEERS, RUN, HEAD_DIM), BF16),
             pltpu.SemaphoreType.DMA((3,)),
@@ -673,9 +719,9 @@
             pltpu.SemaphoreType.DMA((2, 4, 2, PARTS)),
         ],
         compiler_params=pltpu.CompilerParams(
-            collective_id=1, has_side_effects=True, vmem_limit_bytes=12 * 1024 * 1024
+            collective_id=1, has_side_effects=True, vmem_limit_bytes=24 * 1024 * 1024
         ),
-    )(dq, dk, dv)
+    )(ranks, block_target, dq, dk, dv)
 
 
 def deliver_kernel(*refs):
@@ -699,13 +745,12 @@
 
 
 def on_device(query_rows, key_rows, value_rows, output_grad, block_target, doc_lengths):
-    queries, grads, keys, values, targets, lengths = scatter(
+    queries, grads, keys, values, keys_turned, targets, lengths, ranks = scatter(
         query_rows, output_grad, key_rows, value_rows, block_target.transpose(0, 2, 1), doc_lengths
     )
-    pairs = (GROUP_BLOCKS // 2, RUN, HEAD_DIM)
-    dq, dk, dv = attention(targets, lengths, queries, grads, keys.reshape(pairs), values.reshape(pairs))
-    planes = (PLANES, PEERS, RUN, HEAD_DIM)
-    return deliver(*collect(dq, dk.reshape(planes), dv.reshape(planes)))
+    dq, dk, dv = attention(lengths, ranks, targets, queries, grads, keys, values, keys_turned)
+    blocks = (GROUP_BLOCKS, BLOCK_ROWS, HEAD_DIM)
+    return deliver(*collect(ranks, targets, dq, dk.reshape(blocks), dv.reshape(blocks)))
 
 
 def solution(mesh):

time: 100 us -> 99.7 us (level)
    pallas_call x1, Pallas kernels: 42.3 us -> 48 us  [scatter(): pl.pallas_call(scatter_kernel, name='scatter', out_shape=(wide, wide, pac...]
    pallas_call x1, Pallas kernels: 19.6 us -> 14.2 us  [attention(): pl.pallas_call(attention_kernel, name='attention', out_shape=(jax.ShapeDt...]
where the time goes in v4:
time: 99.7 us
  Pallas kernels  98.8 us (99%)
    pallas_call x1, Pallas kernels, scatter(): pl.pallas_call(scatter_kernel, name='scatter', out_shape=(wide, wide, pac...  48 us
    pallas_call x1, Pallas kernels, collect(): pl.pallas_call(collect_kernel, name='collect', out_shape=(jax.ShapeDtypeS...  35.6 us
    pallas_call x1, Pallas kernels, attention(): pl.pallas_call(attention_kernel, name='attention', out_shape=(jax.ShapeDt...  14.2 us

profile of v4, /device:TPU:1, one launch (start us, length us, event | category | flops | bytes accessed | tf_op | source)
XLA Modules:
  0.0 99.7 jit_solution(8725451384904449945)
XLA Ops:
  0.6 48.0 %scatter.1 = (bf16[32,16,1024]{2,1,0:T(8,128)(2,1)S(1)}, bf16[32,16,1024]{2,1,0:T(8,128)(2,1)S(1)}, bf16[4096,128]{1,0:T(8,128)(2,1)S(1)}, bf16[4096,128]{1,0:T(...) custom-call(bf16[128,4096]{1,0:T(8,128)(2,1)} %q_ref.1, ...), custom_call_target="tpu_custom_call" | custom-call | tf_op jit(solution)/shard_map/scatter/pallas_call | solution.py:287
  48.7 14.2 %attention.1 = (f32[16,128,256]{2,1,0:T(8,128)S(1)}, f32[4096,128]{1,0:T(8,128)S(1)}, f32[4096,128]{1,0:T(8,128)S(1)}) custom-call(s32[1,16]{1,0:T(1,128)S(1)} %get-tuple-element.19.length_ref, s32[8,128]{1,0:T(8,128)S(1)} %get-tuple-element.17.rank_ref, s32[8,16,32]{2,1,0:T(8,128)S(1)} %get-tuple-element.18.target_ref, ...), custom_call_target="tpu_custom_call" | custom-call | tf_op jit(solution)/shard_map/attention/pallas_call | solution.py:523
  62.9 35.6 %collect.1 = (bf16[128,4096]{1,0:T(8,128)(2,1)S(1)}, bf16[128,512]{1,0:T(8,128)(2,1)S(1)}, bf16[128,512]{1,0:T(8,128)(2,1)S(1)}) custom-call(s32[8,128]{1,0:T(8,128)S(1)} %get-tuple-element.17.rank_ref, s32[8,16,32]{2,1,0:T(8,128)S(1)} %get-tuple-element.18.target_ref, f32[16,128,256]{2,1,0:T(8,128)S(1)} %get-tuple-element.25.dq_turned, ...), custom_call_target="tpu_custom_call" | custom-call | tf_op jit(solution)/shard_map/collect/pallas_call | solution.py:699
  98.4 1.1 %deliver.1 = (bf16[128,4096]{1,0:T(8,128)(2,1)}, bf16[128,512]{1,0:T(8,128)(2,1)}, bf16[128,512]{1,0:T(8,128)(2,1)}) custom-call(bf16[128,4096]{1,0:T(8,128)(2,1)S(1)} %get-tuple-element.28.refs_0_, bf16[128,512]{1,0:T(8,128)(2,1)S(1)} %get-tuple-element.29.refs_1_, bf16[128,512]{1,0:T(8,128)(2,1)S(1)} %get-tuple-element.30.refs_2_), custom_call_target="tpu_custom_call" | custom-call | tf_op jit(solution)/shard_map/deliver/pallas_call | solution.py:736

commit v5 on v4

--- a/solution.py
+++ b/solution.py
@@ -59,8 +59,8 @@
 
 
 def target_of(target_ref, group, source, from_plane, which):
-    ctx = lax.rem(lax.div(source, 2), 2) * 16 + lax.rem(source, 2) + from_plane * 2
-    return lax.rem(target_ref[lax.div(source, KV_HEADS), 2 * group + which, ctx], GROUP_BLOCKS)
+    ctx = ((source >> 1) & 1) * 16 + (source & 1) + from_plane * 2
+    return target_ref[source >> 2, 2 * group + which, ctx] & (GROUP_BLOCKS - 1)
 
 
 def greet(group, head, plane):
@@ -195,7 +195,7 @@
         place_of = lax.broadcasted_iota(jnp.int32, (8, 128), 0) * 128 + lane
 
         def invert(source, inverse):
-            slot = lax.rem(me + PEERS - source, PEERS)
+            slot = (me - source) & (PEERS - 1)
             for from_plane in range(PLANES):
                 for which in range(2):
                     block = target_of(target_out, group, source, from_plane, which)
@@ -205,7 +205,7 @@
         table[0] = lax.fori_loop(0, PEERS, invert, jnp.zeros((8, 128), jnp.int32))
 
         def mine(step):
-            return target_of(target_out, group, lax.rem(me + PEERS - lax.div(step, 2), PEERS), plane, lax.rem(step, 2))
+            return target_of(target_out, group, (me - (step >> 1)) & (PEERS - 1), plane, step & 1)
 
         blocks = lax.fori_loop(
             0,
@@ -261,7 +261,7 @@
     def pack(chunk, carry):
         first = chunk * CHUNK_BLOCKS
         rows = pl.ds(pl.multiple_of(chunk * CHUNK, CHUNK), CHUNK)
-        held = [packed_from[lax.div(first + n, 128), lax.rem(first + n, 128)] for n in range(CHUNK_BLOCKS)]
+        held = [packed_from[(first + n) >> 7, (first + n) & 127] for n in range(CHUNK_BLOCKS)]
         keys = jnp.concatenate([half_of(k_out[h >> 6, (h >> 1) & (PEERS - 1)], h & 1) for h in held], axis=0)
         k_pack[rows, :] = keys.astype(BF16)
         k_turned[chunk] = jnp.transpose(keys).astype(BF16)
@@ -353,7 +353,7 @@
     def sort(step, carry):
         rank = rank_ref[0, step]
         query_order[rank] = step
-        query_block[rank] = target_of(target_ref, group, lax.rem(me + PEERS - lax.div(step, 2), PEERS), plane, lax.rem(step, 2))
+        query_block[rank] = target_of(target_ref, group, (me - (step >> 1)) & (PEERS - 1), plane, step & 1)
         return carry
 
     lax.fori_loop(0, PLANE_BLOCKS, sort, 0, unroll=8)
@@ -581,7 +581,7 @@
     def rows_of(n, slot, chunk):
         halves = []
         for which in range(2):
-            block = target_of(target_ref, group, lax.rem(me + PEERS - slot, PEERS), chunk, which)
+            block = target_of(target_ref, group, (me - slot) & (PEERS - 1), chunk, which)
             halves.append(parts[n][block])
         rows = jnp.concatenate(halves, axis=0)
         return rows * SCORE_SCALE if n == 0 else rows

time: 99.7 us -> 96.2 us (0.965)
  Pallas kernels: 98.8 us -> 95.5 us
    pallas_call x1, Pallas kernels: 48 us -> 44.9 us  [scatter(): pl.pallas_call(scatter_kernel, name='scatter', out_shape=(wide, wide, pac...]
where the time goes in v5:
time: 96.2 us; the launch traced here: 96.1 us
  Pallas kernels  95.5 us (99%)
    pallas_call x1, Pallas kernels, scatter(): pl.pallas_call(scatter_kernel, name='scatter', out_shape=(wide, wide, pac...  44.9 us
    pallas_call x1, Pallas kernels, collect(): pl.pallas_call(collect_kernel, name='collect', out_shape=(jax.ShapeDtypeS...  35.3 us
    pallas_call x1, Pallas kernels, attention(): pl.pallas_call(attention_kernel, name='attention', out_shape=(jax.ShapeDt...  14.2 us

profile of v5, /device:TPU:1, one launch (start us, length us, event | category | flops | bytes accessed | tf_op | source)
XLA Modules:
  0.0 96.1 jit_solution(5918280514673349922)
XLA Ops:
  0.6 44.9 %scatter.1 = (bf16[32,16,1024]{2,1,0:T(8,128)(2,1)S(1)}, bf16[32,16,1024]{2,1,0:T(8,128)(2,1)S(1)}, bf16[4096,128]{1,0:T(8,128)(2,1)S(1)}, bf16[4096,128]{1,0:T(...) custom-call(bf16[128,4096]{1,0:T(8,128)(2,1)} %q_ref.1, ...), custom_call_target="tpu_custom_call" | custom-call | tf_op jit(solution)/shard_map/scatter/pallas_call | solution.py:287
  45.6 14.2 %attention.1 = (f32[16,128,256]{2,1,0:T(8,128)S(1)}, f32[4096,128]{1,0:T(8,128)S(1)}, f32[4096,128]{1,0:T(8,128)S(1)}) custom-call(s32[1,16]{1,0:T(1,128)S(1)} %get-tuple-element.19.length_ref, s32[8,128]{1,0:T(8,128)S(1)} %get-tuple-element.17.rank_ref, s32[8,16,32]{2,1,0:T(8,128)S(1)} %get-tuple-element.18.target_ref, ...), custom_call_target="tpu_custom_call" | custom-call | tf_op jit(solution)/shard_map/attention/pallas_call | solution.py:523
  59.7 35.3 %collect.1 = (bf16[128,4096]{1,0:T(8,128)(2,1)S(1)}, bf16[128,512]{1,0:T(8,128)(2,1)S(1)}, bf16[128,512]{1,0:T(8,128)(2,1)S(1)}) custom-call(s32[8,128]{1,0:T(8,128)S(1)} %get-tuple-element.17.rank_ref, s32[8,16,32]{2,1,0:T(8,128)S(1)} %get-tuple-element.18.target_ref, f32[16,128,256]{2,1,0:T(8,128)S(1)} %get-tuple-element.25.dq_turned, ...), custom_call_target="tpu_custom_call" | custom-call | tf_op jit(solution)/shard_map/collect/pallas_call | solution.py:699
  95.1 1.1 %deliver.1 = (bf16[128,4096]{1,0:T(8,128)(2,1)}, bf16[128,512]{1,0:T(8,128)(2,1)}, bf16[128,512]{1,0:T(8,128)(2,1)}) custom-call(bf16[128,4096]{1,0:T(8,128)(2,1)S(1)} %get-tuple-element.28.refs_0_, bf16[128,512]{1,0:T(8,128)(2,1)S(1)} %get-tuple-element.29.refs_1_, bf16[128,512]{1,0:T(8,128)(2,1)S(1)} %get-tuple-element.30.refs_2_), custom_call_target="tpu_custom_call" | custom-call | tf_op jit(solution)/shard_map/deliver/pallas_call | solution.py:736

commit v6 on v5

--- a/solution.py
+++ b/solution.py
@@ -27,7 +27,7 @@
 CHUNK_BLOCKS = CHUNK // BLOCK_ROWS
 FIXED_MAX = 7
 TOGETHER = 2
-UNROLL_PREP = 2
+UNROLL_PREP = 4
 SCORE_SCALE = HEAD_DIM**-0.5
 EXP2_SCALE = SCORE_SCALE * 1.4426950408889634
 PARTS = 4
@@ -50,7 +50,7 @@
 
 
 def device_of(group, head, plane):
-    return {"grp": group, "ctx": (head // 2) * 16 + plane * 2 + head % 2}
+    return {"grp": group, "ctx": lax.div(head, 2) * 16 + plane * 2 + lax.rem(head, 2)}
 
 
 def half_of(pair, which):
@@ -72,7 +72,7 @@
         pl.semaphore_signal(
             barrier,
             inc=1,
-            device_id=device_of(peer // KV_HEADS, lax.rem(peer, KV_HEADS), plane),
+            device_id=device_of(lax.div(peer, KV_HEADS), lax.rem(peer, KV_HEADS), plane),
             device_id_type=MESH,
         )
         return carry
@@ -135,20 +135,20 @@
 
     def send_narrow(step, carry):
         peer = lax.rem(me + step, PEERS)
-        to_group, to_head = peer // KV_HEADS, lax.rem(peer, KV_HEADS)
+        to_group, to_head = lax.div(peer, KV_HEADS), lax.rem(peer, KV_HEADS)
         for n, (src, dst) in enumerate(narrow):
             remote(
                 run_of(src, to_group, to_head, HEAD_DIM),
                 dst.at[plane, step],
                 send_sem.at[n],
-                narrow_recv.at[n, step // PART],
+                narrow_recv.at[n, lax.div(step, PART)],
                 device_of(to_group, to_head, plane),
             ).start()
         return carry
 
     def send_wide(step, carry):
         peer = lax.rem(me + step, PEERS)
-        to_group, to_head = peer // KV_HEADS, lax.rem(peer, KV_HEADS)
+        to_group, to_head = lax.div(peer, KV_HEADS), lax.rem(peer, KV_HEADS)
         for n, (src, dst) in enumerate(wide):
             remote(
                 run_of(src, to_group, to_head, UNIT),
@@ -269,7 +269,7 @@
         v_pack[rows, :] = values.astype(BF16)
         return carry
 
-    lax.fori_loop(0, CHUNKS, pack, 0)
+    lax.fori_loop(0, CHUNKS, pack, 0, unroll=4)
     for n in range(2):
         sent = narrow[n][1].at[0, pl.ds(0, PEERS - 1)]
         remote(sent, sent, send_sem.at[n], narrow_recv.at[n, 0], here).wait_send()
@@ -576,7 +576,7 @@
 
     def owner_of(slot):
         peer = lax.rem(me + PEERS - slot, PEERS)
-        return device_of(peer // KV_HEADS, lax.rem(peer, KV_HEADS), plane)
+        return device_of(lax.div(peer, KV_HEADS), lax.rem(peer, KV_HEADS), plane)
 
     def rows_of(n, slot, chunk):
         halves = []
@@ -642,14 +642,14 @@
                             inbox[way, n, step - 1, slot] = (sum_so_far + rows_of(n, slot, chunk)).astype(BF16)
                             return carry
 
-                        lax.fori_loop(part * PART, (part + 1) * PART, add, 0, unroll=4)
+                        lax.fori_loop(part * PART, (part + 1) * PART, add, 0, unroll=8)
                         ring(way, step, n, part, held).start()
                 if step > 0:
                     wide_after = min(wide_next + 2, PEERS)
                     lax.fori_loop(wide_next, wide_after, send_wide, 0)
                     wide_next = wide_after
         if step == 0:
-            lax.fori_loop(0, TILES, turn, 0)
+            lax.fori_loop(0, TILES, turn, 0, unroll=4)
             put_wide(0)
             own_wide = pltpu.make_async_copy(dq_ref.at[0], home_of(dq_out, UNIT), own_sem.at[2])
             own_wide.start()
@@ -667,7 +667,7 @@
                 total[n, slot] = (rows_of(n, slot, plane) + arrived).astype(BF16)
                 return carry
 
-            lax.fori_loop(part * PART, (part + 1) * PART, sum_up, 0, unroll=4)
+            lax.fori_loop(part * PART, (part + 1) * PART, sum_up, 0, unroll=8)
 
             def send_narrow(slot, carry):
                 remote(

time: 96.2 us -> 95.8 us (level)
  no operation moved by 1% of the time
where the time goes in v6:
time: 95.8 us; the launch traced here: 95.7 us
  Pallas kernels  95.1 us (99%)
    pallas_call x1, Pallas kernels, scatter(): pl.pallas_call(scatter_kernel, name='scatter', out_shape=(wide, wide, pac...  44 us
    pallas_call x1, Pallas kernels, collect(): pl.pallas_call(collect_kernel, name='collect', out_shape=(jax.ShapeDtypeS...  36.3 us
    pallas_call x1, Pallas kernels, attention(): pl.pallas_call(attention_kernel, name='attention', out_shape=(jax.ShapeDt...  13.7 us

profile of v6, /device:TPU:1, one launch (start us, length us, event | category | flops | bytes accessed | tf_op | source)
XLA Modules:
  0.0 95.7 jit_solution(2190513867763246064)
XLA Ops:
  0.6 44.0 %scatter.1 = (bf16[32,16,1024]{2,1,0:T(8,128)(2,1)S(1)}, bf16[32,16,1024]{2,1,0:T(8,128)(2,1)S(1)}, bf16[4096,128]{1,0:T(8,128)(2,1)S(1)}, bf16[4096,128]{1,0:T(...) custom-call(bf16[128,4096]{1,0:T(8,128)(2,1)} %q_ref.1, ...), custom_call_target="tpu_custom_call" | custom-call | tf_op jit(solution)/shard_map/scatter/pallas_call | solution.py:287
  44.6 13.7 %attention.1 = (f32[16,128,256]{2,1,0:T(8,128)S(1)}, f32[4096,128]{1,0:T(8,128)S(1)}, f32[4096,128]{1,0:T(8,128)S(1)}) custom-call(s32[1,16]{1,0:T(1,128)S(1)} %get-tuple-element.19.length_ref, s32[8,128]{1,0:T(8,128)S(1)} %get-tuple-element.17.rank_ref, s32[8,16,32]{2,1,0:T(8,128)S(1)} %get-tuple-element.18.target_ref, ...), custom_call_target="tpu_custom_call" | custom-call | tf_op jit(solution)/shard_map/attention/pallas_call | solution.py:523
  58.3 36.3 %collect.1 = (bf16[128,4096]{1,0:T(8,128)(2,1)S(1)}, bf16[128,512]{1,0:T(8,128)(2,1)S(1)}, bf16[128,512]{1,0:T(8,128)(2,1)S(1)}) custom-call(s32[8,128]{1,0:T(8,128)S(1)} %get-tuple-element.17.rank_ref, s32[8,16,32]{2,1,0:T(8,128)S(1)} %get-tuple-element.18.target_ref, f32[16,128,256]{2,1,0:T(8,128)S(1)} %get-tuple-element.25.dq_turned, ...), custom_call_target="tpu_custom_call" | custom-call | tf_op jit(solution)/shard_map/collect/pallas_call | solution.py:699
  94.6 1.1 %deliver.1 = (bf16[128,4096]{1,0:T(8,128)(2,1)}, bf16[128,512]{1,0:T(8,128)(2,1)}, bf16[128,512]{1,0:T(8,128)(2,1)}) custom-call(bf16[128,4096]{1,0:T(8,128)(2,1)S(1)} %get-tuple-element.28.refs_0_, bf16[128,512]{1,0:T(8,128)(2,1)S(1)} %get-tuple-element.29.refs_1_, bf16[128,512]{1,0:T(8,128)(2,1)S(1)} %get-tuple-element.30.refs_2_), custom_call_target="tpu_custom_call" | custom-call | tf_op jit(solution)/shard_map/deliver/pallas_call | solution.py:736

commit v7 on v6

--- a/solution.py
+++ b/solution.py
@@ -63,7 +63,7 @@
     return target_ref[source >> 2, 2 * group + which, ctx] & (GROUP_BLOCKS - 1)
 
 
-def greet(group, head, plane):
+def greet(group, head, plane, meanwhile=None):
     barrier = pltpu.get_barrier_semaphore()
     me = group * KV_HEADS + head
 
@@ -85,6 +85,8 @@
             device_id=device_of(group, head, lax.rem(plane + by, PLANES)),
             device_id_type=MESH,
         )
+    if meanwhile is not None:
+        meanwhile()
     pl.semaphore_wait(barrier, PEERS - 1 + 2)
 
 
@@ -564,7 +566,6 @@
 ):
     group, head, plane = place()
     me = group * KV_HEADS + head
-    greet(group, head, plane)
     here = device_of(group, head, plane)
     parts = (dk_ref, dv_ref)
     outs = (dk_out, dv_out)
@@ -616,6 +617,19 @@
     def chunk_at(way, step):
         distance = 4 - step
         return lax.rem(plane + (distance if way == 0 else PLANES - distance), PLANES)
+
+    def fill_box(way, n, first, after, chunk):
+        def fill(slot, carry):
+            outbox[way, n, slot] = rows_of(n, slot, chunk).astype(BF16)
+            return carry
+
+        lax.fori_loop(first, after, fill, 0, unroll=4)
+
+    def fill_first():
+        for way in range(2):
+            fill_box(way, way, 0, PEERS, chunk_at(way, 0))
+
+    greet(group, head, plane, fill_first)
 
     for step in range(4):
         for part in range(PARTS):
@@ -626,12 +640,8 @@
                     if step == 0 and n != way:
                         continue
                     if step == 0 or (step == 1 and n != way):
-
-                        def fill(slot, carry):
-                            outbox[way, n, slot] = rows_of(n, slot, chunk).astype(BF16)
-                            return carry
-
-                        lax.fori_loop(part * PART, (part + 1) * PART, fill, 0, unroll=4)
+                        if step == 1:
+                            fill_box(way, n, part * PART, (part + 1) * PART, chunk)
                         ring(way, step, n, part, outbox.at[way, n, piece]).start()
                     else:
                         held = inbox.at[way, n, step - 1, piece]

time: 95.8 us -> 95.4 us (level)
    pallas_call x1, Pallas kernels: 36.3 us -> 35.1 us  [collect(): pl.pallas_call(collect_kernel, name='collect', out_shape=(jax.ShapeDtypeS...]
where the time goes in v7:
time: 95.4 us; the launch traced here: 95 us
  Pallas kernels  94.3 us (99%)
    pallas_call x1, Pallas kernels, scatter(): pl.pallas_call(scatter_kernel, name='scatter', out_shape=(wide, wide, pac...  44 us
    pallas_call x1, Pallas kernels, collect(): pl.pallas_call(collect_kernel, name='collect', out_shape=(jax.ShapeDtypeS...  35.1 us
    pallas_call x1, Pallas kernels, attention(): pl.pallas_call(attention_kernel, name='attention', out_shape=(jax.ShapeDt...  14.2 us

profile of v7, /device:TPU:1, one launch (start us, length us, event | category | flops | bytes accessed | tf_op | source)
XLA Modules:
  0.0 95.0 jit_solution(17146266376108804913)
XLA Ops:
  0.6 44.0 %scatter.1 = (bf16[32,16,1024]{2,1,0:T(8,128)(2,1)S(1)}, bf16[32,16,1024]{2,1,0:T(8,128)(2,1)S(1)}, bf16[4096,128]{1,0:T(8,128)(2,1)S(1)}, bf16[4096,128]{1,0:T(...) custom-call(bf16[128,4096]{1,0:T(8,128)(2,1)} %q_ref.1, ...), custom_call_target="tpu_custom_call" | custom-call | tf_op jit(solution)/shard_map/scatter/pallas_call | solution.py:289
  44.6 14.2 %attention.1 = (f32[16,128,256]{2,1,0:T(8,128)S(1)}, f32[4096,128]{1,0:T(8,128)S(1)}, f32[4096,128]{1,0:T(8,128)S(1)}) custom-call(s32[1,16]{1,0:T(1,128)S(1)} %get-tuple-element.19.length_ref, s32[8,128]{1,0:T(8,128)S(1)} %get-tuple-element.17.rank_ref, s32[8,16,32]{2,1,0:T(8,128)S(1)} %get-tuple-element.18.target_ref, ...), custom_call_target="tpu_custom_call" | custom-call | tf_op jit(solution)/shard_map/attention/pallas_call | solution.py:525
  58.8 35.1 %collect.1 = (bf16[128,4096]{1,0:T(8,128)(2,1)S(1)}, bf16[128,512]{1,0:T(8,128)(2,1)S(1)}, bf16[128,512]{1,0:T(8,128)(2,1)S(1)}) custom-call(s32[8,128]{1,0:T(8,128)S(1)} %get-tuple-element.17.rank_ref, s32[8,16,32]{2,1,0:T(8,128)S(1)} %get-tuple-element.18.target_ref, f32[16,128,256]{2,1,0:T(8,128)S(1)} %get-tuple-element.25.dq_turned, ...), custom_call_target="tpu_custom_call" | custom-call | tf_op jit(solution)/shard_map/collect/pallas_call | solution.py:709
  93.9 1.1 %deliver.1 = (bf16[128,4096]{1,0:T(8,128)(2,1)}, bf16[128,512]{1,0:T(8,128)(2,1)}, bf16[128,512]{1,0:T(8,128)(2,1)}) custom-call(bf16[128,4096]{1,0:T(8,128)(2,1)S(1)} %get-tuple-element.28.refs_0_, bf16[128,512]{1,0:T(8,128)(2,1)S(1)} %get-tuple-element.29.refs_1_, bf16[128,512]{1,0:T(8,128)(2,1)S(1)} %get-tuple-element.30.refs_2_), custom_call_target="tpu_custom_call" | custom-call | tf_op jit(solution)/shard_map/deliver/pallas_call | solution.py:746

commit v8 on v7

--- a/solution.py
+++ b/solution.py
@@ -32,7 +32,7 @@
 EXP2_SCALE = SCORE_SCALE * 1.4426950408889634
 PARTS = 4
 PART = PEERS // PARTS
-WIDE_EARLY = 4
+WIDE_EARLY = 8
 WIDE_EACH = 2
 MESH = pl.DeviceIdType.MESH
 F32 = jnp.float32

time: 95.4 us -> 95.1 us (level)
  no operation moved by 1% of the time
where the time goes in v8:
time: 95.1 us; the launch traced here: 95 us
  Pallas kernels  94.4 us (99%)
    pallas_call x1, Pallas kernels, scatter(): pl.pallas_call(scatter_kernel, name='scatter', out_shape=(wide, wide, pac...  44 us
    pallas_call x1, Pallas kernels, collect(): pl.pallas_call(collect_kernel, name='collect', out_shape=(jax.ShapeDtypeS...  34.4 us
    pallas_call x1, Pallas kernels, attention(): pl.pallas_call(attention_kernel, name='attention', out_shape=(jax.ShapeDt...  14.9 us

profile of v8, /device:TPU:1, one launch (start us, length us, event | category | flops | bytes accessed | tf_op | source)
XLA Modules:
  0.0 95.0 jit_solution(13821572442036079292)
XLA Ops:
  0.6 44.0 %scatter.1 = (bf16[32,16,1024]{2,1,0:T(8,128)(2,1)S(1)}, bf16[32,16,1024]{2,1,0:T(8,128)(2,1)S(1)}, bf16[4096,128]{1,0:T(8,128)(2,1)S(1)}, bf16[4096,128]{1,0:T(...) custom-call(bf16[128,4096]{1,0:T(8,128)(2,1)} %q_ref.1, ...), custom_call_target="tpu_custom_call" | custom-call | tf_op jit(solution)/shard_map/scatter/pallas_call | solution.py:289
  44.6 14.9 %attention.1 = (f32[16,128,256]{2,1,0:T(8,128)S(1)}, f32[4096,128]{1,0:T(8,128)S(1)}, f32[4096,128]{1,0:T(8,128)S(1)}) custom-call(s32[1,16]{1,0:T(1,128)S(1)} %get-tuple-element.19.length_ref, s32[8,128]{1,0:T(8,128)S(1)} %get-tuple-element.17.rank_ref, s32[8,16,32]{2,1,0:T(8,128)S(1)} %get-tuple-element.18.target_ref, ...), custom_call_target="tpu_custom_call" | custom-call | tf_op jit(solution)/shard_map/attention/pallas_call | solution.py:525
  59.5 34.4 %collect.1 = (bf16[128,4096]{1,0:T(8,128)(2,1)S(1)}, bf16[128,512]{1,0:T(8,128)(2,1)S(1)}, bf16[128,512]{1,0:T(8,128)(2,1)S(1)}) custom-call(s32[8,128]{1,0:T(8,128)S(1)} %get-tuple-element.17.rank_ref, s32[8,16,32]{2,1,0:T(8,128)S(1)} %get-tuple-element.18.target_ref, f32[16,128,256]{2,1,0:T(8,128)S(1)} %get-tuple-element.25.dq_turned, ...), custom_call_target="tpu_custom_call" | custom-call | tf_op jit(solution)/shard_map/collect/pallas_call | solution.py:709
  93.9 1.1 %deliver.1 = (bf16[128,4096]{1,0:T(8,128)(2,1)}, bf16[128,512]{1,0:T(8,128)(2,1)}, bf16[128,512]{1,0:T(8,128)(2,1)}) custom-call(bf16[128,4096]{1,0:T(8,128)(2,1)S(1)} %get-tuple-element.28.refs_0_, bf16[128,512]{1,0:T(8,128)(2,1)S(1)} %get-tuple-element.29.refs_1_, bf16[128,512]{1,0:T(8,128)(2,1)S(1)} %get-tuple-element.30.refs_2_), custom_call_target="tpu_custom_call" | custom-call | tf_op jit(solution)/shard_map/deliver/pallas_call | solution.py:746
